TPU v7x, 256 devices: a whole 4x4x8 slice. The times are simulated.
256 devices in a mesh: dp: 8 (over x_lo, y), ctx: 32 (over x_hi, z, core).
Axes of the slice: x: 4 (x_hi: 2, x_lo: 2; x = x_hi * 2 + x_lo), y: 4, z: 8, core: 2. Of those that a mesh axis runs over, the one named last changes fastest.
Arguments:
- signal: bfloat16 [8, 256, 16384], P('dp', None, 'ctx'), may hold values from -6 to 6
- grad_out: bfloat16 [8, 256, 16384], P('dp', None, 'ctx'), may hold values from -6 to 6
- residue: float32 [16, 16], replicated, may hold values from -1.5 to 1.5
- decay: float32 [16, 16], replicated, may hold values from 3.0517578e-05 to 0.05
Outputs:
- grad_signal: bfloat16 [8, 256, 16384], P('dp', None, 'ctx')
- grad_residue: float32 [16, 16], replicated
- decay_projection: float32 [16, 16], replicated
All inputs are finite; a program needn't handle non-finite values.
Results may differ from a plain program's by a relative error of at most 0.00105.
Values may be sent and summed in bfloat16 or wider, within the bound.
A program may use at most 64 MiB of HBM per device.

v0:
```python
import math

import jax
import jax.numpy as jnp
from jax import lax
from jax.sharding import PartitionSpec as P

HIGH = lax.Precision.HIGHEST


def mode_basis(decay, positions):
    norm = jnp.sqrt(-jnp.expm1(-2.0 * decay))
    return jnp.exp(-decay[:, :, None] * positions[None, None, :]) * norm[:, :, None]


def angles(index, period):
    return 2.0 * math.pi * (index % period).astype(jnp.float32) / period


def small_forward(stacked, cos_small, sin_small):
    y_re = jnp.einsum("rab,ak->rkb", stacked, cos_small, precision=HIGH)
    y_im = -jnp.einsum("rab,ak->rkb", stacked, sin_small, precision=HIGH)
    return (y_re, y_im)


def twist_forward(y_re, y_im, tw_cos, tw_sin):
    return (y_re * tw_cos + y_im * tw_sin, y_im * tw_cos - y_re * tw_sin)


def twist_back(u_re, u_im, tw_cos, tw_sin):
    return (u_re * tw_cos - u_im * tw_sin, u_im * tw_cos + u_re * tw_sin)


def big_forward(z_re, z_im, cos_big, sin_big):
    x_re = jnp.einsum("rkb,bm->rkm", z_re, cos_big, precision=HIGH) + jnp.einsum(
        "rkb,bm->rkm", z_im, sin_big, precision=HIGH
    )
    x_im = jnp.einsum("rkb,bm->rkm", z_im, cos_big, precision=HIGH) - jnp.einsum(
        "rkb,bm->rkm", z_re, sin_big, precision=HIGH
    )
    return (x_re, x_im)


def big_inverse(s_re, s_im, cos_big, sin_big):
    u_re = jnp.einsum("rkm,mb->rkb", s_re, cos_big, precision=HIGH) - jnp.einsum(
        "rkm,mb->rkb", s_im, sin_big, precision=HIGH
    )
    u_im = jnp.einsum("rkm,mb->rkb", s_im, cos_big, precision=HIGH) + jnp.einsum(
        "rkm,mb->rkb", s_re, sin_big, precision=HIGH
    )
    return (u_re, u_im)


def small_inverse(v_re, v_im, cos_small, sin_small, total):
    in_time = jnp.einsum("rkb,ak->rab", v_re, cos_small, precision=HIGH) - jnp.einsum(
        "rkb,ak->rab", v_im, sin_small, precision=HIGH
    )
    return in_time / total


def spectral_products(x_re, x_im, rows, batch_local, chans, bins, width):
    sig_re = x_re[:rows].reshape(batch_local, chans, bins, width)
    sig_im = x_im[:rows].reshape(batch_local, chans, bins, width)
    grd_re = x_re[rows : 2 * rows].reshape(batch_local, chans, bins, width)
    grd_im = x_im[rows : 2 * rows].reshape(batch_local, chans, bins, width)
    flt_re = x_re[2 * rows :][None]
    flt_im = x_im[2 * rows :][None]
    prod_re = jnp.sum(grd_re * sig_re + grd_im * sig_im, axis=0)
    prod_im = jnp.sum(grd_im * sig_re - grd_re * sig_im, axis=0)
    back_re = (grd_re * flt_re + grd_im * flt_im).reshape(rows, bins, width)
    back_im = (grd_im * flt_re - grd_re * flt_im).reshape(rows, bins, width)
    return (jnp.stack([prod_re, prod_im]), jnp.stack([back_re, back_im]))


def project(group_grad, decay, basis, positions):
    plain_part = jnp.einsum("gs,gms->gm", group_grad, basis, precision=HIGH)
    weighted_part = decay * jnp.einsum(
        "gs,gms->gm", group_grad * positions[None, :], basis, precision=HIGH
    )
    return (plain_part, weighted_part)


def on_device(signal, grad_out, residue, decay):
    parts = lax.axis_size("ctx")
    here = lax.axis_index("ctx")
    batch_local, chans, width = signal.shape
    groups = residue.shape[0]
    per_group = chans // groups
    total = 2 * parts * width
    full = jnp.arange(width, dtype=jnp.int32)
    block_ids = jnp.arange(parts, dtype=jnp.int32)
    freq_ids = jnp.arange(2 * parts, dtype=jnp.int32)
    group_ids = jnp.arange(groups, dtype=jnp.int32)
    small_angle = angles(block_ids[:, None] * freq_ids[None, :], 2 * parts)
    cos_small = jnp.cos(small_angle)
    sin_small = jnp.sin(small_angle)
    big_angle = angles(full[:, None] * full[None, :], width)
    cos_big = jnp.cos(big_angle)
    sin_big = jnp.sin(big_angle)
    scale = 1.0 / math.sqrt(per_group * lax.axis_size("dp") * batch_local * parts * width)
    step = width // parts
    rows = batch_local * chans
    span = jnp.arange(step, dtype=jnp.int32)
    slice_pos = here * step + span
    sent = (
        lax.all_to_all(
            signal.reshape(rows, 1, width), "ctx", split_axis=2, concat_axis=1, tiled=True
        ),
        lax.all_to_all(
            grad_out.reshape(rows, 1, width), "ctx", split_axis=2, concat_axis=1, tiled=True
        ),
    )
    spread_pos = (
        (block_ids[:, None] * width + slice_pos[None, :]).astype(jnp.float32).reshape(parts * step)
    )
    spread_basis = mode_basis(decay, spread_pos)
    filt = jnp.einsum("gm,gmn->gn", residue, spread_basis, precision=HIGH)
    filt = jnp.repeat(filt, per_group, axis=0).reshape(chans, parts, step)
    stacked = jnp.concatenate(
        [sent[0].astype(jnp.float32), sent[1].astype(jnp.float32), filt], axis=0
    )
    y_re, y_im = small_forward(stacked, cos_small, sin_small)
    twist = angles(freq_ids[:, None] * slice_pos[None, :], total)
    z_re, z_im = twist_forward(y_re, y_im, jnp.cos(twist), jnp.sin(twist))
    moved = lax.all_to_all(jnp.stack([z_re, z_im]), "ctx", split_axis=2, concat_axis=3, tiled=True)
    x_re, x_im = big_forward(moved[0], moved[1], cos_big, sin_big)
    local_sum, back = spectral_products(x_re, x_im, rows, batch_local, chans, 2, width)
    summed = lax.psum(local_sum, "dp")
    owned = summed.shape[1]
    spectra = jnp.concatenate([back, summed], axis=1)
    u_re, u_im = big_inverse(spectra[0], spectra[1], cos_big, sin_big)
    owned_freq = 2 * here + jnp.arange(2, dtype=jnp.int32)
    turn = angles(owned_freq[:, None] * full[None, :], total)
    v_re, v_im = twist_back(u_re, u_im, jnp.cos(turn), jnp.sin(turn))
    returned = lax.all_to_all(
        jnp.stack([v_re, v_im]), "ctx", split_axis=3, concat_axis=2, tiled=True
    )
    in_time = small_inverse(returned[0], returned[1], cos_small, sin_small, total)
    located = lax.all_to_all(in_time, "ctx", split_axis=1, concat_axis=2, tiled=True).reshape(
        rows + owned, width
    )
    grad_signal = located[:rows].reshape(batch_local, chans, width).astype(jnp.bfloat16)
    filter_grad = located[rows:]
    owner = jnp.arange(owned, dtype=jnp.int32) // per_group
    onehot = (owner[:, None] == group_ids[None, :]).astype(jnp.float32)
    group_grad = jnp.einsum("cg,cs->gs", onehot, filter_grad, precision=HIGH)
    positions = (here * width + full).astype(jnp.float32)
    basis = mode_basis(decay, positions)
    plain_part, weighted_part = project(group_grad, decay, basis, positions)
    plain_sum, weighted_sum = lax.psum((plain_part, weighted_part), "ctx")
    return (grad_signal, plain_sum * scale, weighted_sum * scale)


def solution(mesh):
    placed = (P("dp", None, "ctx"), P("dp", None, "ctx"), P(), P())
    return jax.shard_map(
        on_device,
        mesh=mesh,
        in_specs=placed,
        out_specs=(P("dp", None, "ctx"), P(), P()),
        check_vma=False,
    )
```

profile of v0, /device:TPU:1, one launch (start us, length us, event | category | flops | bytes accessed | tf_op | source)
XLA Modules:
  0.0 675.5 jit_solution(17749826381141937863)
XLA Ops:
  7.2 1.3 copy.45
  9.0 2.3 reduce.1
  11.3 0.8 reshape.249
  12.1 12.6 %all-to-all-start = ((bf16[32,2,2048]{2,1,0:T(2,128)(2,1)}), bf16[32,2,2048]{2,1,0:T(2,128)(2,1)S(1)}, u32[]{:S(2)}, u32[]{:S(2)}) async-start(bf16[32,2,2048]{2,1,0:T(2,128)(2,1)} %reshape.249), calls=%async_computation | async-start | bytes 524288 | tf_op jit(solution)/shard_map/all_to_all | solution.py:106
  24.7 1.3 copy.47
  26.0 2.3 reduce
  28.2 0.8 reshape.247
  29.0 9.0 %all-to-all-done = bf16[32,2,2048]{2,1,0:T(2,128)(2,1)S(1)} async-done(((bf16[32,2,2048]{2,1,0:T(2,128)(2,1)}), bf16[32,2,2048]{2,1,0:T(2,128)(2,1)S(1)}, u32[]{:S(2)}, u32[]{:S(2)}) %all-to-all-start) | async-done | bytes 262176 | tf_op jit(solution)/shard_map/all_to_all | solution.py:106
  38.1 5.0 all-to-all-start.1
  43.9 2.8 reshape_reshape.3
  46.7 3.8 copy.51
  51.1 5.6 all-to-all-done.1
  56.6 0.7 reshape.248
  57.5 2.8 fusion.8
  60.3 3.4 add_bitcast_fusion
  64.4 3.6 copy.52
  68.1 144.4 %all_to_all.57 = f32[2,768,64,16]{1,3,0,2:T(8,128)S(1)} all-to-all(f32[2,768,64,16]{1,3,0,2:T(8,128)S(1)} %copy.52), channel_id=1, replica_groups=mesh['dp'=8,'ctx'=32] {'ctx'}, dimensions={2} | all-to-all | bytes 12582912 | tf_op jit(solution)/shard_map/all_to_all | solution.py:125
  213.0 0.8 fusion.137
  214.1 9.3 %fusion.21 = f32[768,2,512]{2,0,1:T(8,128)S(1)} fusion(f32[768,2,512]{0,2,1:T(8,128)S(1)} %bitcast.116), kind=kOutput, calls=%fused_computation.38 | convolution fusion | flops 4835508224 | bytes 6291456 | tf_op jit(solution)/shard_map/rkb,bm->rkm/dot_general | solution.py:35
  223.5 9.5 %fusion.19 = f32[768,2,512]{2,0,1:T(8,128)S(1)} fusion(f32[768,2,512]{0,2,1:T(8,128)S(1)} %bitcast.118), kind=kOutput, calls=%fused_computation.36 | convolution fusion | flops 4835508224 | bytes 6291456 | tf_op jit(solution)/shard_map/rkb,bm->rkm/dot_general | solution.py:38
  233.0 9.8 %convolution_add_fusion = f32[768,2,512]{2,0,1:T(8,128)S(1)} fusion(f32[768,2,512]{2,0,1:T(8,128)S(1)} %fusion.21, f32[768,2,512]{0,2,1:T(8,128)S(1)} %bitcast.119), kind=kOutput, calls=%fused_computation.15 | convolution fusion | flops 4836294656 | bytes 9437184 | tf_op jit(solution)/shard_map/rkb,bm->rkm/dot_general | solution.py:35
  242.9 9.6 %convolution_subtract_fusion = f32[768,2,512]{2,0,1:T(8,128)S(1)} fusion(f32[768,2,512]{2,0,1:T(8,128)S(1)} %fusion.19, f32[768,2,512]{0,2,1:T(8,128)S(1)} %bitcast.117), kind=kOutput, calls=%fused_computation.14 | convolution fusion | flops 4836294656 | bytes 9437184 | tf_op jit(solution)/shard_map/rkb,bm->rkm/dot_general | solution.py:38
  252.5 0.8 add_bitcast_fusion.3
  253.4 1.5 pad_maximum_fusion.3
  255.1 80.8 %all-reduce.3.cloned.1.call-done = f32[2,256,2,512]{3,1,2,0:T(8,128)} async-done(((f32[2,256,2,512]{3,1,2,0:T(8,128)}), f32[2,256,2,512]{3,1,2,0:T(8,128)}) %all-reduce.3.cloned.1.call-update) | async-done | bytes 2097168 | tf_op jit(solution)/shard_map/psum | solution.py:128
  335.9 2.0 pad_maximum_fusion.1
  337.9 7.3 %fusion.1 = f32[512,2,512]{2,0,1:T(8,128)S(1)} fusion(f32[2,512,2,512]{3,1,2,0:T(8,128)S(1)} %pad_maximum_fusion.1), kind=kOutput, calls=%fused_computation.11 | convolution fusion | flops 3224895488 | bytes 4194304 | tf_op jit(solution)/shard_map/rkm,mb->rkb/dot_general | solution.py:45
  345.2 7.7 %fusion = f32[512,2,512]{2,0,1:T(8,128)S(1)} fusion(f32[2,512,2,512]{3,1,2,0:T(8,128)S(1)} %pad_maximum_fusion.1), kind=kOutput, calls=%fused_computation.10 | convolution fusion | flops 3224895488 | bytes 4194304 | tf_op jit(solution)/shard_map/rkm,mb->rkb/dot_general | solution.py:48
  353.0 7.5 %fusion.4 = f32[512,2,512]{2,0,1:T(8,128)S(1)} fusion(f32[512,2,512]{2,0,1:T(8,128)S(1)} %fusion.1, f32[2,512,2,512]{3,1,2,0:T(8,128)S(1)} %pad_maximum_fusion.1), kind=kOutput, calls=%fused_computation.16 | convolution fusion | flops 3225419776 | bytes 6291456 | tf_op jit(solution)/shard_map/rkm,mb->rkb/dot_general | solution.py:45
  360.6 7.8 %subtract_bitcast_fusion.1 = (f32[1,512,2,512]{3,1,2,0:T(8,128)S(1)}, f32[1,512,2,512]{3,1,2,0:T(8,128)S(1)}) fusion(f32[512,2,512]{2,0,1:T(8,128)S(1)} %fusion.4, f32[2,512]{1,0:T(2,128)S(1)} %get-tuple-element.29, f32[2,512]{1,0:T(2,128)S(1)} %get-tuple-element.28, f32[512,2,512]{2,0,1:T(8,128)S(1)} %fusion, f32[2,512,2,512]{3,1,2,0:T(8,128)S(1)} %pad_maximum_fusion.1), kind=kOutput, calls=%fused_computation.9 | convolution fusion | flops 3228565504 | bytes 10493952 | tf_op jit(solution)/shard_map/rkm,mb->rkb/dot_general | solution.py:48
  368.4 2.4 pad_maximum_fusion.2
  370.8 7.3 %copy.60 = f32[2,512,2,512]{1,2,0,3:T(2,128)} copy(f32[2,512,2,512]{3,1,2,0:T(8,128)} %pad_maximum_fusion.2) | data formatting | bytes 8388608 | tf_op jit(solution)/shard_map/stack | solution.py:136
  378.1 108.7 %all_to_all.58 = f32[2,512,2,512]{1,2,0,3:T(2,128)S(1)} all-to-all(f32[2,512,2,512]{1,2,0,3:T(2,128)} %copy.60), channel_id=1, replica_groups=mesh['dp'=8,'ctx'=32] {'ctx'}, dimensions={3} | all-to-all | bytes 8388608 | tf_op jit(solution)/shard_map/all_to_all | solution.py:135
  486.8 1.3 copy.61
  488.2 2.0 fusion.138
  490.2 1.6 copy.62
  491.8 2.5 squeeze.22
  494.3 2.9 fusion.62
  497.2 2.9 copy.63
  500.2 2.7 squeeze.23
  502.9 1.2 fusion.7
  504.1 1.6 copy.64
  505.7 6.2 all-to-all-start.4
  511.9 27.7 %all-to-all-done.4 = f32[512,32,16]{0,2,1:T(8,128)S(1)} async-done(((f32[512,32,16]{0,2,1:T(8,128)}), f32[512,32,16]{0,2,1:T(8,128)S(1)}, u32[]{:S(2)}, u32[]{:S(2)}) %all-to-all-start.4) | async-done | bytes 1048608 | tf_op jit(solution)/shard_map/all_to_all | solution.py:139
  540.1 0.8 fusion.26
  540.9 0.8 fusion.27
  541.7 0.8 copy.65
  542.6 125.2 %all-reduce = (f32[16,16]{1,0:T(8,128)S(1)}, f32[16,16]{1,0:T(8,128)S(1)}) all-reduce(f32[16,16]{1,0:T(8,128)S(1)} %bitcast.133, f32[16,16]{1,0:T(8,128)S(1)} %mul.350), channel_id=1, replica_groups=mesh['dp'=8,'ctx'=32] {'ctx'}, use_global_device_ids=true, to_apply=%region_1.2 | all-reduce | flops 512 | bytes 4096 | tf_op jit(solution)/shard_map/psum | solution.py:150
  (39 shorter events, 4.9 us)
Async XLA Ops:
  7.2 36.1 %copy-start = (f32[16,16]{1,0:T(8,128)S(1)}, f32[16,16]{1,0:T(8,128)}, u32[]{:S(2)}) copy-start(f32[16,16]{1,0:T(8,128)} %param.6) | copy-start | bytes 3076
  7.2 21.8 %copy-start.3 = (f32[16,16]{1,0:T(8,128)S(1)}, f32[16,16]{1,0:T(8,128)}, u32[]{:S(2)}) copy-start(f32[16,16]{1,0:T(8,128)} %param.7) | copy-start | bytes 3076
  12.1 26.0 %all-to-all-start = ((bf16[32,2,2048]{2,1,0:T(2,128)(2,1)}), bf16[32,2,2048]{2,1,0:T(2,128)(2,1)S(1)}, u32[]{:S(2)}, u32[]{:S(2)}) async-start(bf16[32,2,2048]{2,1,0:T(2,128)(2,1)} %reshape.249), calls=%async_computation | async-start | bytes 524288 | tf_op jit(solution)/shard_map/all_to_all | solution.py:106
  38.1 18.6 %all-to-all-start.1 = ((bf16[32,2,2048]{2,1,0:T(2,128)(2,1)}), bf16[32,2,2048]{2,1,0:T(2,128)(2,1)S(1)}, u32[]{:S(2)}, u32[]{:S(2)}) async-start(bf16[32,2,2048]{2,1,0:T(2,128)(2,1)} %reshape.247), calls=%async_computation.1 | async-start | bytes 524288 | tf_op jit(solution)/shard_map/all_to_all | solution.py:109
  43.1 292.8 %all-reduce.3.cloned.1.call-start = ((), (), s32[]{:S(2)}) async-start(), calls=%async_computation.5 | async-start | bytes 4194304 | tf_op jit(solution)/shard_map/psum | solution.py:128
  494.3 2.9 copy-start.2
  504.1 164.3 %copy-start.1 = (f32[16,16]{1,0:T(8,128)S(1)}, f32[16,16]{1,0:T(8,128)}, u32[]{:S(2)}) copy-start(f32[16,16]{1,0:T(8,128)} %param.6) | copy-start | bytes 3076
  505.7 34.0 %all-to-all-start.4 = ((f32[512,32,16]{0,2,1:T(8,128)}), f32[512,32,16]{0,2,1:T(8,128)S(1)}, u32[]{:S(2)}, u32[]{:S(2)}) async-start(f32[512,32,16]{0,2,1:T(8,128)} %copy.64), calls=%async_computation.4 | async-start | bytes 2097152 | tf_op jit(solution)/shard_map/all_to_all | solution.py:139
Sparse Core Ops, SparseCore 0:
  255.0 80.8 all-reduce.2
where the time goes:
time: 686 us; the launch traced here: 675 us
  blocking collectives  378 us (55%)
  waiting for transfers between devices  123 us (18%)
  matrix products  81.5 us (12%)
  local copies, waits for them, and re-layouts  40.9 us (6%)
  starting transfers between devices  23.9 us (3%)
  between operations  14.7 us (2%)
  other arithmetic  13 us (2%)
    all_to_all x1, blocking collectives, on_device(): lax.all_to_all(jnp.stack([z_re, z_im]), 'ctx', split_axis=2, concat_axis=...  144 us
    psum x1, blocking collectives, on_device(): plain_sum, weighted_sum = lax.psum((plain_part, weighted_part), 'ctx')  125 us
    all_to_all x1, blocking collectives, on_device(): lax.all_to_all(jnp.stack([v_re, v_im]), 'ctx', split_axis=3, concat_axis=...  109 us
    psum x1, waiting for transfers between devices, on_device(): summed = lax.psum(local_sum, 'dp')  80.8 us
    all_to_all x1, waiting for transfers between devices, on_device(): lax.all_to_all(in_time, 'ctx', split_axis=1, concat_axis=2, tiled=True)  27.7 us
  transfers between devices with their start and end apart: 4, of which 4 were waited for; matrix products, arithmetic and copies ran while one was open for 2% of the time, Pallas kernels for 0%

commit v1 on v0

v1 whole, which is shorter than its diff:
```python
import functools
import math

import jax
import jax.numpy as jnp
from jax import lax
from jax.experimental import pallas as pl
from jax.experimental.pallas import tpu as pltpu
from jax.sharding import PartitionSpec as P

MESH = pl.DeviceIdType.MESH
F32 = jnp.float32
BF16 = jnp.bfloat16
LANES = 128
HIGH = lax.Precision.HIGHEST


def iota(shape, dim):
    return lax.broadcasted_iota(jnp.int32, shape, dim)


def split(value):
    top = value.astype(BF16)
    return top, (value - top.astype(F32)).astype(BF16)


def wrap(value, size):
    return jnp.where(value >= size, value - size, value)


def down(value, rows):
    return jnp.concatenate([value[rows:], jnp.zeros((rows, value.shape[1]), value.dtype)], axis=0)


def nt(left, right):
    return lax.dot_general(left, right, (((1,), (1,)), ((), ())), preferred_element_type=F32)


def tn(left, right):
    return lax.dot_general(left, right, (((0,), (0,)), ((), ())), preferred_element_type=F32)


def nn(left, right):
    return jnp.dot(left, right, preferred_element_type=F32)


def all_wait(ref, sem):
    pltpu.make_async_copy(ref, ref, sem).wait()


def kernel(
    dims, x_hbm, g_hbm, res_hbm, dec_hbm, out_hbm, p_hbm, q_hbm,
    xv, gv, resv, decv, dcol, rcol, lg, lx, fwd, bwd, yg, yx, wout, hrow, xrev, lagv, outl, rx, outv, pv, qv,
    send1, recv1, sendl, recvl, send2, recv2, send3, recv3,
    in_sem, out_sem, s1, r1, sl, rl, s2, r2, s3, r3,
):
    parts, batch, groups, modes, per_group, width, scale = dims
    rows = groups * modes
    chunks = width // LANES
    me = lax.axis_index("ctx")
    row_of = lax.axis_index("dp")

    loads = []
    for i, (src, dst) in enumerate(
        ((dec_hbm, decv), (res_hbm, resv), (g_hbm.at[0], gv), (x_hbm.at[0], xv))
    ):
        loads.append(pltpu.make_async_copy(src, dst, in_sem.at[i]))
        loads[-1].start()
    barrier = pltpu.get_barrier_semaphore()
    for i in range(1, parts):
        pl.semaphore_signal(barrier, inc=1, device_id={"ctx": wrap(me + i, parts)}, device_id_type=MESH)
    for i in range(1, batch):
        pl.semaphore_signal(barrier, inc=1, device_id={"dp": wrap(row_of + i, batch)}, device_id_type=MESH)

    loads[0].wait()
    loads[1].wait()
    dec = decv[...]
    series = dec * dec
    series = 1.0 + series / 6.0 * (1.0 + series / 20.0 * (1.0 + series / 42.0 * (1.0 + series / 72.0)))
    norm = jnp.sqrt(2.0 * jnp.exp(-dec) * dec * series)
    eye = iota((modes, modes), 0) == iota((modes, modes), 1)
    for g in range(groups):
        at = slice(g * modes, (g + 1) * modes)
        for src, dst in ((dec, dcol), (resv[...] * norm, rcol)):
            column = jnp.sum(jnp.where(eye, src[g : g + 1, :], 0.0), axis=1, keepdims=True)
            dst[at, :] = jnp.broadcast_to(column, (modes, LANES))

    lane_pos = iota((modes, width), 1).astype(F32)
    back_pos = width - lane_pos
    for g in range(groups):
        at = slice(g * modes, (g + 1) * modes)
        second = slice(rows + g * modes, rows + (g + 1) * modes)
        d = jnp.concatenate([dcol[at, :]] * chunks, axis=1)
        for pos, keep, dst in ((lane_pos, fwd, lg), (back_pos, bwd, lx)):
            e = jnp.exp(-(d * pos))
            keep[at, :] = e
            dst[at, :width], dst[at, width:] = split(e)
            dst[second, :width], dst[second, width:] = split(e * pos)

    loads[2].wait()
    yg[...] = nt(lg[...], jnp.concatenate([gv[...], gv[...]], axis=1))
    loads[3].wait()
    yx[...] = nt(lx[...], jnp.concatenate([xv[...], xv[...]], axis=1))

    segment = iota((8, LANES), 1) // per_group
    own_segment = segment == iota((8, LANES), 0)
    turned_segment = [segment == (iota((8, LANES), 0) + seg) % 8 for seg in range(8)]
    for k in range(parts):
        first = (k * 8 // modes) * per_group
        half, seg = first // LANES, (first % LANES) // per_group
        for kind, src in enumerate((yg, yg, yx, yx)):
            r0 = (kind % 2) * rows + k * 8
            v = src[r0 : r0 + 8, half * LANES : (half + 1) * LANES]
            v = pltpu.roll(v, 0, axis=1, stride=per_group, stride_axis=0)
            send1[k, kind : kind + 1, :] = jnp.sum(jnp.where(turned_segment[seg], v, 0.0), axis=0, keepdims=True)

    pl.semaphore_wait(barrier, parts - 1 + batch - 1)
    for i in range(1, parts):
        to = wrap(me + i, parts)
        pltpu.make_async_remote_copy(
            src_ref=send1.at[to], dst_ref=recv1.at[me], send_sem=s1, recv_sem=r1,
            device_id={"ctx": to}, device_id_type=MESH,
        ).start()
    recv1[pl.ds(me, 1)] = send1[pl.ds(me, 1)]

    anti = (iota((LANES, LANES), 0) + iota((LANES, LANES), 1) == LANES - 1).astype(BF16)
    for i in range(chunks):
        at = slice(i * LANES, (i + 1) * LANES)
        xrev[:, at] = nn(xv[:, at], anti).astype(BF16)
    lane = iota((LANES, LANES), 1)
    sub = iota((LANES, LANES), 0)
    later = lane >= sub
    low = iota((modes, LANES), 1) % per_group < per_group // 2
    for g in range(groups):
        at = slice(g * per_group, (g + 1) * per_group)
        left = jnp.concatenate([gv[at, j * LANES : (j + 1) * LANES] for j in range(chunks)], axis=0)
        right = jnp.concatenate(
            [
                jnp.concatenate(
                    [
                        xrev[at, (j - b) * LANES : (j - b + 1) * LANES] if b <= j else jnp.zeros((per_group, LANES), BF16)
                        for b in range(chunks)
                    ],
                    axis=1,
                )
                for j in range(chunks)
            ],
            axis=0,
        )
        pairs = tn(left, right)
        turned = [
            pltpu.roll(pairs[:, b * LANES : (b + 1) * LANES], 0, axis=1, stride=1, stride_axis=0)
            for b in range(chunks)
        ]
        zero = jnp.zeros((LANES, LANES), F32)
        for b in range(chunks + 1):
            here = turned[b] if b < chunks else zero
            before = turned[b - 1] if b > 0 else zero
            lagv[g : g + 1, b * LANES : (b + 1) * LANES] = jnp.sum(jnp.where(later, here, before), axis=0, keepdims=True)
    zero_lane = iota((groups, LANES), 1) == 0
    lags = [pltpu.roll(lagv[:, b * LANES : (b + 1) * LANES], 1, axis=1) for b in range(chunks + 1)]
    lags = jnp.concatenate([jnp.where(zero_lane, lags[b], lags[b + 1]) for b in range(chunks)], axis=1)
    for g in range(groups):
        at = slice(g * modes, (g + 1) * modes)
        e = fwd[at, :] * lags[g : g + 1, :]
        w = e * lane_pos
        e = sum(e[:, b * LANES : (b + 1) * LANES] for b in range(chunks))
        w = sum(w[:, b * LANES : (b + 1) * LANES] for b in range(chunks))
        for shift in (64, 32, 16, 8):
            e = e + pltpu.roll(e, shift, axis=1)
            w = w + pltpu.roll(w, shift, axis=1)
        both = jnp.where(low, e, w)
        for h in range(modes // 8):
            k = g * (modes // 8) + h
            sendl[k] = jnp.sum(jnp.where(own_segment, both[h * 8 : (h + 1) * 8], 0.0), axis=0, keepdims=True)
    for i in range(1, parts):
        to = wrap(me + i, parts)
        pltpu.make_async_remote_copy(
            src_ref=sendl.at[to], dst_ref=recvl.at[me], send_sem=sl, recv_sem=rl,
            device_id={"ctx": to}, device_id_type=MESH,
        ).start()
    recvl[pl.ds(me, 1)] = sendl[pl.ds(me, 1)]

    mine = dcol[pl.ds(pl.multiple_of(me * 8, 8), 8), :]
    seg = me * 8 // modes % (LANES // per_group)
    dl = jnp.sum(jnp.where(segment == (iota((8, LANES), 0) + seg) % 8, mine, 0.0), axis=0, keepdims=True)
    all_wait(recv1.at[pl.ds(0, parts - 1)], r1)
    gs, gt, xs, xt = (recv1[:, kind, :] for kind in range(4))
    n = 1
    while n < parts:
        factor = jnp.exp(-(dl * float(n * width)))
        ahead = down(gs, n)
        gt = gt + factor * (down(gt, n) + float(n * width) * ahead)
        gs = gs + factor * ahead
        n *= 2
    gs, gt = down(gs, 1), down(gt, 1)
    for p in range(parts):
        send2[p, 0:1, :] = gs[p : p + 1, :]
    plain = jnp.sum(xs * gs, axis=0, keepdims=True)
    weighted = jnp.sum(xs * gt + xt * gs, axis=0, keepdims=True)
    plain = plain + pltpu.roll(plain, LANES - per_group // 2, axis=1)
    weighted = weighted + pltpu.roll(weighted, per_group // 2, axis=1)
    all_wait(recvl.at[pl.ds(0, parts - 1)], rl)
    local = jnp.sum(recvl[...], axis=0)
    first_half = iota((1, LANES), 1) % per_group < per_group // 2
    pair_row = pltpu.roll(jnp.where(first_half, plain, weighted), (8 - seg) % 8 * per_group, axis=1) + local
    for p in range(parts):
        send2[p, 1:2, :] = pair_row
    for i in range(1, parts):
        to = wrap(me + i, parts)
        pltpu.make_async_remote_copy(
            src_ref=send2.at[to], dst_ref=recv2.at[me], send_sem=s2, recv_sem=r2,
            device_id={"ctx": to}, device_id_type=MESH,
        ).start()
    recv2[pl.ds(me, 1)] = send2[pl.ds(me, 1)]

    for g in range(groups):
        at = slice(g * modes, (g + 1) * modes)
        w = jnp.concatenate([rcol[at, :]] * chunks, axis=1) * bwd[at, :]
        wout[at, :], wout[rows + g * modes : rows + (g + 1) * modes, :] = split(w)
        hrow[g : g + 1, :width] = jnp.sum(w, axis=0, keepdims=True)
        start = jnp.sum(rcol[at, :], axis=0, keepdims=True)
        hrow[g : g + 1, width:] = jnp.where(iota((1, LANES), 1) == 0, start, 0.0)
    for g in range(groups):
        at = slice(g * per_group, (g + 1) * per_group)
        turned = [
            pltpu.roll(
                jnp.broadcast_to(hrow[g : g + 1, b * LANES : (b + 1) * LANES], (LANES, LANES)),
                0, axis=1, stride=1, stride_axis=0,
            )
            for b in range(chunks + 1)
        ]
        blocks = [
            jnp.concatenate(split(jnp.where(later, turned[chunks - b], turned[chunks - 1 - b])), axis=1)
            for b in range(chunks)
        ]
        right = jnp.concatenate(blocks, axis=0)
        left = jnp.concatenate(
            [
                gv[at, :] if i == 0 else jnp.concatenate(
                    [gv[at, i * LANES :], jnp.zeros((per_group, i * LANES), BF16)], axis=1
                )
                for i in range(chunks)
            ],
            axis=0,
        )
        o = nn(left, right)
        o = o[:, :LANES] + o[:, LANES:]
        for i in range(chunks):
            outl[at, i * LANES : (i + 1) * LANES] = o[i * per_group : (i + 1) * per_group, :]
    rx[...] = jnp.zeros_like(rx)

    all_wait(recv2.at[pl.ds(0, parts - 1)], r2)
    from_lane, to_lane = iota((LANES, LANES), 0), iota((LANES, LANES), 1)
    same_mode = from_lane // per_group == to_lane % 8
    kind_of = (from_lane % per_group >= per_group // 2) == (to_lane >= LANES // 2)
    select = jnp.where(same_mode & kind_of & (to_lane % (LANES // 2) < modes), 1.0, 0.0)
    sums = jnp.dot(recv2[:, 1, :], select, precision=HIGH, preferred_element_type=F32)
    sums = jnp.where(iota((parts, LANES), 0) % 2 == iota((parts, LANES), 1) % modes // 8, sums, 0.0)
    fold = (iota((groups, parts), 0) == iota((groups, parts), 1) // 2).astype(F32)
    send3[...] = jnp.dot(fold, sums, precision=HIGH, preferred_element_type=F32)
    for i in range(1, batch):
        to = wrap(row_of + i, batch)
        pltpu.make_async_remote_copy(
            src_ref=send3, dst_ref=recv3.at[row_of], send_sem=s3, recv_sem=r3,
            device_id={"dp": to}, device_id_type=MESH,
        ).start()
    recv3[pl.ds(row_of, 1)] = send3[...][None]

    for k in range(parts):
        first = (k * 8 // modes) * per_group
        half, seg = first // LANES, (first % LANES) // per_group
        v = jnp.broadcast_to(recv2[k, 0:1, :], (8, LANES))
        v = jnp.where(turned_segment[seg], v, 0.0)
        for shift in (64, 32, 16):
            v = v + pltpu.roll(v, shift, axis=1)
        v = jnp.where(segment == seg, v, 0.0)
        rx[k * 8 : (k + 1) * 8, half * LANES : (half + 1) * LANES] = v
    r_top, r_low = split(rx[...])
    w_top, w_low = wout[:rows, :], wout[rows:, :]
    far = tn(jnp.concatenate([r_top, r_top, r_low], axis=0), jnp.concatenate([w_top, w_low, w_top], axis=0))
    outv[...] = (outl[...] + far).astype(BF16)
    store = pltpu.make_async_copy(outv, out_hbm.at[0], out_sem.at[0])
    store.start()

    all_wait(recv3.at[pl.ds(0, batch - 1)], r3)
    total = recv3[0]
    for b in range(1, batch):
        total = total + recv3[b]
    pv[...] = total[:, :modes] * (norm * scale)
    qv[...] = total[:, LANES // 2 : LANES // 2 + modes] * (dec * norm * scale)
    more = [pltpu.make_async_copy(pv, p_hbm, out_sem.at[1]), pltpu.make_async_copy(qv, q_hbm, out_sem.at[2])]
    for copy in more:
        copy.start()
    all_wait(send1.at[pl.ds(0, parts - 1)], s1)
    all_wait(sendl.at[pl.ds(0, parts - 1)], sl)
    all_wait(send2.at[pl.ds(0, parts - 1)], s2)
    all_wait(recv3.at[pl.ds(0, batch - 1)], s3)
    store.wait()
    for copy in more:
        copy.wait()


def on_device(parts, batch, signal, grad_out, residue, decay):
    _, chans, width = signal.shape
    groups, modes = residue.shape
    per_group = chans // groups
    rows = groups * modes
    scale = 1.0 / math.sqrt(per_group * batch * parts * width)
    dims = (parts, batch, groups, modes, per_group, width, scale)
    vm = pltpu.VMEM
    return pl.pallas_call(
        functools.partial(kernel, dims),
        out_shape=(
            jax.ShapeDtypeStruct(signal.shape, BF16),
            jax.ShapeDtypeStruct((groups, modes), F32),
            jax.ShapeDtypeStruct((groups, modes), F32),
        ),
        in_specs=[pl.BlockSpec(memory_space=pl.ANY)] * 4,
        out_specs=[pl.BlockSpec(memory_space=pl.ANY)] * 3,
        scratch_shapes=[
            vm((chans, width), BF16), vm((chans, width), BF16), vm((groups, modes), F32), vm((groups, modes), F32),
            vm((rows, LANES), F32), vm((rows, LANES), F32),
            vm((2 * rows, 2 * width), BF16), vm((2 * rows, 2 * width), BF16),
            vm((rows, width), F32), vm((rows, width), F32),
            vm((2 * rows, chans), F32), vm((2 * rows, chans), F32),
            vm((2 * rows, width), BF16), vm((groups, width + LANES), F32),
            vm((chans, width), BF16), vm((groups, width + LANES), F32),
            vm((chans, width), F32), vm((rows, chans), F32), vm((chans, width), BF16),
            vm((groups, modes), F32), vm((groups, modes), F32),
            vm((parts, 4, LANES), F32), vm((parts, 4, LANES), F32),
            vm((parts, 1, LANES), F32), vm((parts, 1, LANES), F32),
            vm((parts, 2, LANES), F32), vm((parts, 2, LANES), F32),
            vm((groups, LANES), F32), vm((batch, groups, LANES), F32),
            pltpu.SemaphoreType.DMA((4,)), pltpu.SemaphoreType.DMA((3,)),
        ] + [pltpu.SemaphoreType.DMA] * 8,
        compiler_params=pltpu.CompilerParams(
            collective_id=0, has_side_effects=True, vmem_limit_bytes=40 * 1024 * 1024
        ),
    )(signal, grad_out, residue, decay)


def solution(mesh):
    placed = (P("dp", None, "ctx"), P("dp", None, "ctx"), P(), P())
    return jax.shard_map(
        functools.partial(on_device, mesh.shape["ctx"], mesh.shape["dp"]),
        mesh=mesh,
        in_specs=placed,
        out_specs=(P("dp", None, "ctx"), P(), P()),
        check_vma=False,
    )
```

time: 686 us -> 35.8 us (0.05); the launches traced: 675 us -> 35.6 us
  blocking collectives: 378 us -> 0 us
  waiting for transfers between devices: 123 us -> 0 us
  matrix products: 81.5 us -> 0 us
  local copies, waits for them, and re-layouts: 40.9 us -> 5.19 us
  Pallas kernels: 0 us -> 29.7 us
  starting transfers between devices: 23.9 us -> 0 us
  between operations: 14.7 us -> 0.65 us
  other arithmetic: 13 us -> 0 us
    all_to_all x2 -> x0, blocking collectives: 253 us -> none  [the longest x1 144 us: on_device(): lax.all_to_all(jnp.stack([z_re, z_im]), 'ctx', split_axis=2, concat_axis=...]
    psum x1 -> x0, blocking collectives: 125 us -> none  [on_device(): plain_sum, weighted_sum = lax.psum((plain_part, weighted_part), 'ctx')]
    dot_general x16 -> x0, matrix products: 81.5 us -> none  [the longest x1 9.84 us: big_forward(): jnp.einsum('rkb,bm->rkm', z_im, sin_big, precision=HIGH)]
    psum x1 -> x0, waiting for transfers between devices: 80.8 us -> none  [on_device(): summed = lax.psum(local_sum, 'dp')]
    all_to_all x3 -> x0, waiting for transfers between devices: 42.3 us -> none  [the longest x1 27.7 us: on_device(): lax.all_to_all(in_time, 'ctx', split_axis=1, concat_axis=2, tiled=True)]
    pallas_call x0 -> x1, Pallas kernels: none -> 29.7 us  [on_device(): pl.pallas_call(functools.partial(kernel, dims), out_shape=(jax.ShapeDtype...]
    all_to_all x3 -> x0, starting transfers between devices: 23.8 us -> none  [the longest x1 12.6 us: on_device(): lax.all_to_all(signal.reshape(rows, 1, width), 'ctx', split_axis=2, conca...]
    another operation x4 -> x0, local copies, waits for them, and re-layouts: 17.5 us -> none  [the longest x1 7.33 us: on_device(): jnp.stack([v_re, v_im])]
  transfers between devices with their start and end apart: 4 -> 0, of which waited for: 4 -> 0; matrix products, arithmetic and copies ran while one was open for 2% -> 0% of each run, Pallas kernels for 0% -> 0%
where the time goes in v1:
time: 35.8 us; the launch traced here: 35.6 us
  Pallas kernels  29.7 us (83%)
  local copies, waits for them, and re-layouts  5.19 us (14%)
  between operations  0.65 us (2%)
    pallas_call x1, Pallas kernels, on_device(): pl.pallas_call(functools.partial(kernel, dims), out_shape=(jax.ShapeDtype...  29.7 us
    unnamed x11, local copies, waits for them, and re-layouts  5.19 us

profile of v1, /device:TPU:1, one launch (start us, length us, event | category | flops | bytes accessed | tf_op | source)
XLA Modules:
  0.0 35.6 jit_solution(3078789753334165535)
XLA Ops:
  0.6 0.0 copy-start
  0.6 0.9 %copy-done = bf16[1,256,512]{2,1,0:T(8,128)(2,1)S(1)} copy-done((bf16[1,256,512]{2,1,0:T(8,128)(2,1)S(1)}, bf16[1,256,512]{2,1,0:T(8,128)(2,1)}, u32[]{:S(2)}) %copy-start) | copy-done | bytes 262168
  1.6 0.0 copy-start.1
  1.6 0.9 %copy-done.1 = bf16[1,256,512]{2,1,0:T(8,128)(2,1)S(1)} copy-done((bf16[1,256,512]{2,1,0:T(8,128)(2,1)S(1)}, bf16[1,256,512]{2,1,0:T(8,128)(2,1)}, u32[]{:S(2)}) %copy-start.1) | copy-done | bytes 262168
  2.5 0.0 copy-start.2
  2.5 0.7 %copy-done.2 = f32[16,16]{1,0:T(8,128)S(1)} copy-done((f32[16,16]{1,0:T(8,128)S(1)}, f32[16,16]{1,0:T(8,128)}, u32[]{:S(2)}) %copy-start.2) | copy-done | bytes 1048
  3.2 0.0 copy-start.3
  3.2 0.7 %copy-done.3 = f32[16,16]{1,0:T(8,128)S(1)} copy-done((f32[16,16]{1,0:T(8,128)S(1)}, f32[16,16]{1,0:T(8,128)}, u32[]{:S(2)}) %copy-start.3) | copy-done | bytes 1048
  3.9 29.7 %shard_map.67 = (bf16[1,256,512]{2,1,0:T(8,128)(2,1)S(1)}, f32[16,16]{1,0:T(8,128)S(1)}, f32[16,16]{1,0:T(8,128)S(1)}) custom-call(bf16[1,256,512]{2,1,0:T(8,128)(2,1)S(1)} %copy-done, bf16[1,256,512]{2,1,0:T(8,128)(2,1)S(1)} %copy-done.1, f32[16,16]{1,0:T(8,128)S(1)} %copy-done.2, f32[16,16]{1,0:T(8,128)S(1)} %copy-done.3), custom_call_target="tpu_custom_call" | custom-call | tf_op jit(solution)/shard_map/pallas_call | solution.py:312
  33.7 0.7 %copy.10 = bf16[1,256,512]{2,1,0:T(8,128)(2,1)} copy(bf16[1,256,512]{2,1,0:T(8,128)(2,1)S(1)} %get-tuple-element.6) | data formatting | bytes 524288
  34.4 0.6 %copy.11 = f32[16,16]{1,0:T(8,128)} copy(f32[16,16]{1,0:T(8,128)S(1)} %get-tuple-element.7) | data formatting | bytes 2048
  35.0 0.6 %copy.12 = f32[16,16]{1,0:T(8,128)} copy(f32[16,16]{1,0:T(8,128)S(1)} %get-tuple-element.8) | data formatting | bytes 2048
Async XLA Ops:
  0.6 1.0 %copy-start = (bf16[1,256,512]{2,1,0:T(8,128)(2,1)S(1)}, bf16[1,256,512]{2,1,0:T(8,128)(2,1)}, u32[]{:S(2)}) copy-start(bf16[1,256,512]{2,1,0:T(8,128)(2,1)} %x_hbm.1) | copy-start | bytes 786436
  1.6 0.9 %copy-start.1 = (bf16[1,256,512]{2,1,0:T(8,128)(2,1)S(1)}, bf16[1,256,512]{2,1,0:T(8,128)(2,1)}, u32[]{:S(2)}) copy-start(bf16[1,256,512]{2,1,0:T(8,128)(2,1)} %g_hbm.1) | copy-start | bytes 786436
  2.5 0.7 %copy-start.2 = (f32[16,16]{1,0:T(8,128)S(1)}, f32[16,16]{1,0:T(8,128)}, u32[]{:S(2)}) copy-start(f32[16,16]{1,0:T(8,128)} %res_hbm.1) | copy-start | bytes 3076
  3.2 0.7 %copy-start.3 = (f32[16,16]{1,0:T(8,128)S(1)}, f32[16,16]{1,0:T(8,128)}, u32[]{:S(2)}) copy-start(f32[16,16]{1,0:T(8,128)} %dec_hbm.1) | copy-start | bytes 3076

commit v2 on v1

--- a/solution.py
+++ b/solution.py
@@ -12,6 +12,7 @@
 F32 = jnp.float32
 BF16 = jnp.bfloat16
 LANES = 128
+OWNERS = 4
 HIGH = lax.Precision.HIGHEST
 
 
@@ -48,17 +49,45 @@
     pltpu.make_async_copy(ref, ref, sem).wait()
 
 
+def greet(barrier, axis, me, size):
+    for i in range(1, size):
+        pl.semaphore_signal(barrier, inc=1, device_id={axis: wrap(me + i, size)}, device_id_type=MESH)
+
+
+def send(src, dst, send_sem, recv_sem, axis, to):
+    pltpu.make_async_remote_copy(
+        src_ref=src, dst_ref=dst, send_sem=send_sem, recv_sem=recv_sem, device_id={axis: to}, device_id_type=MESH
+    ).start()
+
+
+def scatter(src_of, dst, send_sem, recv_sem, axis, me, size):
+    for i in range(1, size):
+        to = wrap(me + i, size)
+        send(src_of(to), dst, send_sem, recv_sem, axis, to)
+
+
 def kernel(
-    dims, x_hbm, g_hbm, res_hbm, dec_hbm, out_hbm, p_hbm, q_hbm,
-    xv, gv, resv, decv, dcol, rcol, lg, lx, fwd, bwd, yg, yx, wout, hrow, xrev, lagv, outl, rx, outv, pv, qv,
-    send1, recv1, sendl, recvl, send2, recv2, send3, recv3,
-    in_sem, out_sem, s1, r1, sl, rl, s2, r2, s3, r3,
+    dims, x_hbm, g_hbm, res_hbm, dec_hbm, outv, pv, qv,
+    xv, gv, resv, decv, dcol, rcol, lg, lx, fwd, bwd, yg, yx, wout, hrow, xrev, lagv, outl, rx,
+    send1, recv1, sendl, recvl, send2, recv2, send3, recv3, send4, recv4,
+    in_sem, s1, r1, sl, rl, s2, r2, s3, r3, s4, r4,
 ):
     parts, batch, groups, modes, per_group, width, scale = dims
     rows = groups * modes
     chunks = width // LANES
     me = lax.axis_index("ctx")
     row_of = lax.axis_index("dp")
+    owners, share = recv2.shape[0], recv2.shape[1]
+    run = owners // 2
+    owner_ids = [o // run * (parts // 2) + o % run for o in range(owners)]
+    slot = me // (parts // 2) * run + me % (parts // 2)
+    is_owner = me % (parts // 2) < run
+    plain = jnp.logical_not(is_owner)
+
+    def gather(src, dst, send_sem, recv_sem):
+        for o, to in enumerate(owner_ids):
+            pl.when(me != to)(functools.partial(send, src.at[o], dst.at[me], send_sem, recv_sem, "ctx", to))
+
 
     loads = []
     for i, (src, dst) in enumerate(
@@ -67,10 +96,11 @@
         loads.append(pltpu.make_async_copy(src, dst, in_sem.at[i]))
         loads[-1].start()
     barrier = pltpu.get_barrier_semaphore()
-    for i in range(1, parts):
-        pl.semaphore_signal(barrier, inc=1, device_id={"ctx": wrap(me + i, parts)}, device_id_type=MESH)
-    for i in range(1, batch):
-        pl.semaphore_signal(barrier, inc=1, device_id={"dp": wrap(row_of + i, batch)}, device_id_type=MESH)
+
+    @pl.when(is_owner)
+    def _():
+        greet(barrier, "ctx", me, parts)
+        greet(barrier, "dp", row_of, batch)
 
     loads[0].wait()
     loads[1].wait()
@@ -112,16 +142,11 @@
             r0 = (kind % 2) * rows + k * 8
             v = src[r0 : r0 + 8, half * LANES : (half + 1) * LANES]
             v = pltpu.roll(v, 0, axis=1, stride=per_group, stride_axis=0)
-            send1[k, kind : kind + 1, :] = jnp.sum(jnp.where(turned_segment[seg], v, 0.0), axis=0, keepdims=True)
-
-    pl.semaphore_wait(barrier, parts - 1 + batch - 1)
-    for i in range(1, parts):
-        to = wrap(me + i, parts)
-        pltpu.make_async_remote_copy(
-            src_ref=send1.at[to], dst_ref=recv1.at[me], send_sem=s1, recv_sem=r1,
-            device_id={"ctx": to}, device_id_type=MESH,
-        ).start()
-    recv1[pl.ds(me, 1)] = send1[pl.ds(me, 1)]
+            send1[k // share, k % share, kind : kind + 1, :] = jnp.sum(jnp.where(turned_segment[seg], v, 0.0), axis=0, keepdims=True)
+
+    pl.when(is_owner)(lambda: pl.semaphore_wait(barrier, owners - 1 + batch - 1))
+    pl.when(plain)(lambda: pl.semaphore_wait(barrier, owners))
+    gather(send1, recv1, s1, r1)
 
     anti = (iota((LANES, LANES), 0) + iota((LANES, LANES), 1) == LANES - 1).astype(BF16)
     for i in range(chunks):
@@ -172,47 +197,8 @@
         both = jnp.where(low, e, w)
         for h in range(modes // 8):
             k = g * (modes // 8) + h
-            sendl[k] = jnp.sum(jnp.where(own_segment, both[h * 8 : (h + 1) * 8], 0.0), axis=0, keepdims=True)
-    for i in range(1, parts):
-        to = wrap(me + i, parts)
-        pltpu.make_async_remote_copy(
-            src_ref=sendl.at[to], dst_ref=recvl.at[me], send_sem=sl, recv_sem=rl,
-            device_id={"ctx": to}, device_id_type=MESH,
-        ).start()
-    recvl[pl.ds(me, 1)] = sendl[pl.ds(me, 1)]
-
-    mine = dcol[pl.ds(pl.multiple_of(me * 8, 8), 8), :]
-    seg = me * 8 // modes % (LANES // per_group)
-    dl = jnp.sum(jnp.where(segment == (iota((8, LANES), 0) + seg) % 8, mine, 0.0), axis=0, keepdims=True)
-    all_wait(recv1.at[pl.ds(0, parts - 1)], r1)
-    gs, gt, xs, xt = (recv1[:, kind, :] for kind in range(4))
-    n = 1
-    while n < parts:
-        factor = jnp.exp(-(dl * float(n * width)))
-        ahead = down(gs, n)
-        gt = gt + factor * (down(gt, n) + float(n * width) * ahead)
-        gs = gs + factor * ahead
-        n *= 2
-    gs, gt = down(gs, 1), down(gt, 1)
-    for p in range(parts):
-        send2[p, 0:1, :] = gs[p : p + 1, :]
-    plain = jnp.sum(xs * gs, axis=0, keepdims=True)
-    weighted = jnp.sum(xs * gt + xt * gs, axis=0, keepdims=True)
-    plain = plain + pltpu.roll(plain, LANES - per_group // 2, axis=1)
-    weighted = weighted + pltpu.roll(weighted, per_group // 2, axis=1)
-    all_wait(recvl.at[pl.ds(0, parts - 1)], rl)
-    local = jnp.sum(recvl[...], axis=0)
-    first_half = iota((1, LANES), 1) % per_group < per_group // 2
-    pair_row = pltpu.roll(jnp.where(first_half, plain, weighted), (8 - seg) % 8 * per_group, axis=1) + local
-    for p in range(parts):
-        send2[p, 1:2, :] = pair_row
-    for i in range(1, parts):
-        to = wrap(me + i, parts)
-        pltpu.make_async_remote_copy(
-            src_ref=send2.at[to], dst_ref=recv2.at[me], send_sem=s2, recv_sem=r2,
-            device_id={"ctx": to}, device_id_type=MESH,
-        ).start()
-    recv2[pl.ds(me, 1)] = send2[pl.ds(me, 1)]
+            sendl[k // share, k % share : k % share + 1, :] = jnp.sum(jnp.where(own_segment, both[h * 8 : (h + 1) * 8], 0.0), axis=0, keepdims=True)
+    gather(sendl, recvl, sl, rl)
 
     for g in range(groups):
         at = slice(g * modes, (g + 1) * modes)
@@ -250,27 +236,53 @@
             outl[at, i * LANES : (i + 1) * LANES] = o[i * per_group : (i + 1) * per_group, :]
     rx[...] = jnp.zeros_like(rx)
 
-    all_wait(recv2.at[pl.ds(0, parts - 1)], r2)
-    from_lane, to_lane = iota((LANES, LANES), 0), iota((LANES, LANES), 1)
-    same_mode = from_lane // per_group == to_lane % 8
-    kind_of = (from_lane % per_group >= per_group // 2) == (to_lane >= LANES // 2)
-    select = jnp.where(same_mode & kind_of & (to_lane % (LANES // 2) < modes), 1.0, 0.0)
-    sums = jnp.dot(recv2[:, 1, :], select, precision=HIGH, preferred_element_type=F32)
-    sums = jnp.where(iota((parts, LANES), 0) % 2 == iota((parts, LANES), 1) % modes // 8, sums, 0.0)
-    fold = (iota((groups, parts), 0) == iota((groups, parts), 1) // 2).astype(F32)
-    send3[...] = jnp.dot(fold, sums, precision=HIGH, preferred_element_type=F32)
-    for i in range(1, batch):
-        to = wrap(row_of + i, batch)
-        pltpu.make_async_remote_copy(
-            src_ref=send3, dst_ref=recv3.at[row_of], send_sem=s3, recv_sem=r3,
-            device_id={"dp": to}, device_id_type=MESH,
-        ).start()
-    recv3[pl.ds(row_of, 1)] = send3[...][None]
+    @pl.when(is_owner)
+    def _():
+        recv1[pl.ds(me, 1)] = send1[pl.ds(slot, 1)]
+        recvl[pl.ds(me, 1)] = sendl[pl.ds(slot, 1)]
+        all_wait(recv1.at[pl.ds(0, parts - 1)], r1)
+        first_half = iota((1, LANES), 1) % per_group < per_group // 2
+        for j in range(share):
+            k = slot * share + j
+            seg = k * 8 // modes % (LANES // per_group)
+            mine = dcol[pl.ds(pl.multiple_of(k * 8, 8), 8), :]
+            dl = jnp.sum(jnp.where(segment == (iota((8, LANES), 0) + seg) % 8, mine, 0.0), axis=0, keepdims=True)
+            gs, gt, xs, xt = (recv1[:, j, kind, :] for kind in range(4))
+            n = 1
+            while n < parts:
+                factor = jnp.exp(-(dl * float(n * width)))
+                ahead = down(gs, n)
+                gt = gt + factor * (down(gt, n) + float(n * width) * ahead)
+                gs = gs + factor * ahead
+                n *= 2
+            gs, gt = down(gs, 1), down(gt, 1)
+            send2[:, j, :] = gs
+            one = jnp.sum(xs * gs, axis=0, keepdims=True)
+            two = jnp.sum(xs * gt + xt * gs, axis=0, keepdims=True)
+            one = one + pltpu.roll(one, LANES - per_group // 2, axis=1)
+            two = two + pltpu.roll(two, per_group // 2, axis=1)
+            send3[j : j + 1, :] = pltpu.roll(jnp.where(first_half, one, two), (8 - seg) % 8 * per_group, axis=1)
+        recv2[pl.ds(slot, 1)] = send2[pl.ds(me, 1)]
+        all_wait(recvl.at[pl.ds(0, parts - 1)], rl)
+        send3[...] = send3[...] + jnp.sum(recvl[...], axis=0)
+        recv3[pl.ds(row_of, 1)] = send3[...][None]
+        scatter(lambda to: send3, recv3.at[row_of], s3, r3, "dp", row_of, batch)
+        scatter(lambda to: send2.at[to], recv2.at[slot], s2, r2, "ctx", me, parts)
+        all_wait(recv3.at[pl.ds(0, batch - 1)], r3)
+        total = recv3[0]
+        for b in range(1, batch):
+            total = total + recv3[b]
+        send4[...] = total
+        recv4[pl.ds(slot, 1)] = total[None]
+        scatter(lambda to: send4, recv4.at[slot], s4, r4, "ctx", me, parts)
+        all_wait(recv2.at[pl.ds(0, owners - 1)], r2)
+
+    pl.when(plain)(lambda: all_wait(recv2, r2))
 
     for k in range(parts):
         first = (k * 8 // modes) * per_group
         half, seg = first // LANES, (first % LANES) // per_group
-        v = jnp.broadcast_to(recv2[k, 0:1, :], (8, LANES))
+        v = jnp.broadcast_to(recv2[k // share, k % share : k % share + 1, :], (8, LANES))
         v = jnp.where(turned_segment[seg], v, 0.0)
         for shift in (64, 32, 16):
             v = v + pltpu.roll(v, shift, axis=1)
@@ -279,26 +291,34 @@
     r_top, r_low = split(rx[...])
     w_top, w_low = wout[:rows, :], wout[rows:, :]
     far = tn(jnp.concatenate([r_top, r_top, r_low], axis=0), jnp.concatenate([w_top, w_low, w_top], axis=0))
-    outv[...] = (outl[...] + far).astype(BF16)
-    store = pltpu.make_async_copy(outv, out_hbm.at[0], out_sem.at[0])
-    store.start()
-
-    all_wait(recv3.at[pl.ds(0, batch - 1)], r3)
-    total = recv3[0]
-    for b in range(1, batch):
-        total = total + recv3[b]
+    outv[0] = (outl[...] + far).astype(BF16)
+
+    from_lane, to_lane = iota((LANES, LANES), 0), iota((LANES, LANES), 1)
+    same_mode = from_lane // per_group == to_lane % 8
+    kind_of = (from_lane % per_group >= per_group // 2) == (to_lane >= LANES // 2)
+    select = jnp.where(same_mode & kind_of & (to_lane % (LANES // 2) < modes), 1.0, 0.0)
+    fold = (iota((groups, parts), 0) == iota((groups, parts), 1) // 2).astype(F32)
+    pl.when(is_owner)(lambda: all_wait(recv4.at[pl.ds(0, owners - 1)], r4))
+    pl.when(plain)(lambda: all_wait(recv4, r4))
+    sums = jnp.concatenate([recv4[o] for o in range(owners)], axis=0)
+    sums = jnp.dot(sums, select, precision=HIGH, preferred_element_type=F32)
+    sums = jnp.where(iota((parts, LANES), 0) % 2 == iota((parts, LANES), 1) % modes // 8, sums, 0.0)
+    total = jnp.dot(fold, sums, precision=HIGH, preferred_element_type=F32)
     pv[...] = total[:, :modes] * (norm * scale)
     qv[...] = total[:, LANES // 2 : LANES // 2 + modes] * (dec * norm * scale)
-    more = [pltpu.make_async_copy(pv, p_hbm, out_sem.at[1]), pltpu.make_async_copy(qv, q_hbm, out_sem.at[2])]
-    for copy in more:
-        copy.start()
-    all_wait(send1.at[pl.ds(0, parts - 1)], s1)
-    all_wait(sendl.at[pl.ds(0, parts - 1)], sl)
-    all_wait(send2.at[pl.ds(0, parts - 1)], s2)
-    all_wait(recv3.at[pl.ds(0, batch - 1)], s3)
-    store.wait()
-    for copy in more:
-        copy.wait()
+
+    @pl.when(is_owner)
+    def _():
+        all_wait(send1.at[pl.ds(0, owners - 1)], s1)
+        all_wait(sendl.at[pl.ds(0, owners - 1)], sl)
+        all_wait(send2.at[pl.ds(0, parts - 1)], s2)
+        all_wait(recv3.at[pl.ds(0, batch - 1)], s3)
+        all_wait(recvl.at[pl.ds(0, parts - 1)], s4)
+
+    @pl.when(plain)
+    def _():
+        all_wait(send1, s1)
+        all_wait(sendl, sl)
 
 
 def on_device(parts, batch, signal, grad_out, residue, decay):
@@ -307,17 +327,20 @@
     per_group = chans // groups
     rows = groups * modes
     scale = 1.0 / math.sqrt(per_group * batch * parts * width)
+    owners = OWNERS
+    share = rows // 8 // owners
     dims = (parts, batch, groups, modes, per_group, width, scale)
     vm = pltpu.VMEM
+    shapes = (
+        jax.ShapeDtypeStruct(signal.shape, BF16),
+        jax.ShapeDtypeStruct((groups, modes), F32),
+        jax.ShapeDtypeStruct((groups, modes), F32),
+    )
     return pl.pallas_call(
         functools.partial(kernel, dims),
-        out_shape=(
-            jax.ShapeDtypeStruct(signal.shape, BF16),
-            jax.ShapeDtypeStruct((groups, modes), F32),
-            jax.ShapeDtypeStruct((groups, modes), F32),
-        ),
+        out_shape=tuple(vm(shape.shape, shape.dtype) for shape in shapes),
         in_specs=[pl.BlockSpec(memory_space=pl.ANY)] * 4,
-        out_specs=[pl.BlockSpec(memory_space=pl.ANY)] * 3,
+        out_specs=[pl.BlockSpec(memory_space=vm)] * 3,
         scratch_shapes=[
             vm((chans, width), BF16), vm((chans, width), BF16), vm((groups, modes), F32), vm((groups, modes), F32),
             vm((rows, LANES), F32), vm((rows, LANES), F32),
@@ -326,16 +349,16 @@
             vm((2 * rows, chans), F32), vm((2 * rows, chans), F32),
             vm((2 * rows, width), BF16), vm((groups, width + LANES), F32),
             vm((chans, width), BF16), vm((groups, width + LANES), F32),
-            vm((chans, width), F32), vm((rows, chans), F32), vm((chans, width), BF16),
-            vm((groups, modes), F32), vm((groups, modes), F32),
-            vm((parts, 4, LANES), F32), vm((parts, 4, LANES), F32),
-            vm((parts, 1, LANES), F32), vm((parts, 1, LANES), F32),
-            vm((parts, 2, LANES), F32), vm((parts, 2, LANES), F32),
-            vm((groups, LANES), F32), vm((batch, groups, LANES), F32),
-            pltpu.SemaphoreType.DMA((4,)), pltpu.SemaphoreType.DMA((3,)),
-        ] + [pltpu.SemaphoreType.DMA] * 8,
+            vm((chans, width), F32), vm((rows, chans), F32),
+            vm((owners, share, 4, LANES), F32), vm((parts, share, 4, LANES), F32),
+            vm((owners, share, LANES), F32), vm((parts, share, LANES), F32),
+            vm((parts, share, LANES), F32), vm((owners, share, LANES), F32),
+            vm((share, LANES), F32), vm((batch, share, LANES), F32),
+            vm((share, LANES), F32), vm((owners, share, LANES), F32),
+            pltpu.SemaphoreType.DMA((4,)),
+        ] + [pltpu.SemaphoreType.DMA] * 10,
         compiler_params=pltpu.CompilerParams(
-            collective_id=0, has_side_effects=True, vmem_limit_bytes=40 * 1024 * 1024
+            collective_id=0, has_side_effects=True, vmem_limit_bytes=60 * 1024 * 1024
         ),
     )(signal, grad_out, residue, decay)
 

time: 35.8 us -> 31.9 us (0.89)
  local copies, waits for them, and re-layouts: 5.19 us -> 1.9 us
  Pallas kernels: 29.7 us -> 29.3 us
    unnamed x11 -> x3, local copies, waits for them, and re-layouts: 5.19 us -> 1.9 us
    pallas_call x1, Pallas kernels: 29.7 us -> 29.3 us  [on_device(): pl.pallas_call(functools.partial(kernel, dims), out_shape=tuple((vm(shape...]
where the time goes in v2:
time: 31.9 us; the launch traced here: 31.8 us
  Pallas kernels  29.3 us (92%)
  local copies, waits for them, and re-layouts  1.9 us (6%)
  between operations  0.64 us (2%)
    pallas_call x1, Pallas kernels, on_device(): pl.pallas_call(functools.partial(kernel, dims), out_shape=tuple((vm(shape...  29.3 us
    unnamed x3, local copies, waits for them, and re-layouts  1.9 us

profile of v2, /device:TPU:1, one launch (start us, length us, event | category | flops | bytes accessed | tf_op | source)
XLA Modules:
  0.0 31.8 jit_solution(6320603252505892393)
XLA Ops:
  0.6 29.3 %shard_map.67 = (bf16[1,256,512]{2,1,0:T(8,128)(2,1)S(1)}, f32[16,16]{1,0:T(8,128)S(1)}, f32[16,16]{1,0:T(8,128)S(1)}) custom-call(bf16[1,256,512]{2,1,0:T(8,128)(2,1)} %x_hbm.1, bf16[1,256,512]{2,1,0:T(8,128)(2,1)} %g_hbm.1, f32[16,16]{1,0:T(8,128)} %res_hbm.1, f32[16,16]{1,0:T(8,128)} %dec_hbm.1), custom_call_target="tpu_custom_call" | custom-call | tf_op jit(solution)/shard_map/pallas_call | solution.py:339
  29.9 0.7 %copy.10 = bf16[1,256,512]{2,1,0:T(8,128)(2,1)} copy(bf16[1,256,512]{2,1,0:T(8,128)(2,1)S(1)} %get-tuple-element.3) | data formatting | bytes 524288
  30.6 0.6 %copy.11 = f32[16,16]{1,0:T(8,128)} copy(f32[16,16]{1,0:T(8,128)S(1)} %get-tuple-element.4) | data formatting | bytes 2048
  31.2 0.6 %copy.12 = f32[16,16]{1,0:T(8,128)} copy(f32[16,16]{1,0:T(8,128)S(1)} %get-tuple-element.5) | data formatting | bytes 2048

commit v3 on v2

--- a/solution.py
+++ b/solution.py
@@ -321,6 +321,14 @@
         all_wait(sendl, sl)
 
 
+def finish(*refs):
+    copies = [pltpu.make_async_copy(refs[i], refs[3 + i], refs[6].at[i]) for i in range(3)]
+    for copy in copies:
+        copy.start()
+    for copy in copies:
+        copy.wait()
+
+
 def on_device(parts, batch, signal, grad_out, residue, decay):
     _, chans, width = signal.shape
     groups, modes = residue.shape
@@ -336,7 +344,7 @@
         jax.ShapeDtypeStruct((groups, modes), F32),
         jax.ShapeDtypeStruct((groups, modes), F32),
     )
-    return pl.pallas_call(
+    results = pl.pallas_call(
         functools.partial(kernel, dims),
         out_shape=tuple(vm(shape.shape, shape.dtype) for shape in shapes),
         in_specs=[pl.BlockSpec(memory_space=pl.ANY)] * 4,
@@ -361,6 +369,14 @@
             collective_id=0, has_side_effects=True, vmem_limit_bytes=60 * 1024 * 1024
         ),
     )(signal, grad_out, residue, decay)
+    return pl.pallas_call(
+        finish,
+        out_shape=shapes,
+        in_specs=[pl.BlockSpec(memory_space=vm)] * 3,
+        out_specs=[pl.BlockSpec(memory_space=pl.ANY)] * 3,
+        scratch_shapes=[pltpu.SemaphoreType.DMA((3,))],
+        compiler_params=pltpu.CompilerParams(vmem_limit_bytes=4 * 1024 * 1024),
+    )(*results)
 
 
 def solution(mesh):

time: 31.9 us -> 30.8 us (0.966)
  local copies, waits for them, and re-layouts: 1.9 us -> 0 us
  Pallas kernels: 29.3 us -> 30 us
    unnamed x3 -> x0, local copies, waits for them, and re-layouts: 1.9 us -> none
    pallas_call x0 -> x1, Pallas kernels: none -> 0.74 us  [on_device(): pl.pallas_call(finish, out_shape=shapes, in_specs=[pl.BlockSpec(memory_sp...]
where the time goes in v3:
time: 30.8 us; the launch traced here: 30.6 us
  Pallas kernels  30 us (97%)
  between operations  0.64 us (2%)
    pallas_call x1, Pallas kernels, on_device(): pl.pallas_call(functools.partial(kernel, dims), out_shape=tuple((vm(shape...  29.3 us
    pallas_call x1, Pallas kernels, on_device(): pl.pallas_call(finish, out_shape=shapes, in_specs=[pl.BlockSpec(memory_sp...  0.74 us

profile of v3, /device:TPU:1, one launch (start us, length us, event | category | flops | bytes accessed | tf_op | source)
XLA Modules:
  0.0 30.6 jit_solution(10392343960155413685)
XLA Ops:
  0.6 29.3 %shard_map.67 = (bf16[1,256,512]{2,1,0:T(8,128)(2,1)S(1)}, f32[16,16]{1,0:T(8,128)S(1)}, f32[16,16]{1,0:T(8,128)S(1)}) custom-call(bf16[1,256,512]{2,1,0:T(8,128)(2,1)} %x_hbm.1, bf16[1,256,512]{2,1,0:T(8,128)(2,1)} %g_hbm.1, f32[16,16]{1,0:T(8,128)} %res_hbm.1, f32[16,16]{1,0:T(8,128)} %dec_hbm.1), custom_call_target="tpu_custom_call" | custom-call | tf_op jit(solution)/shard_map/pallas_call | solution.py:347
  29.9 0.7 %shard_map.68 = (bf16[1,256,512]{2,1,0:T(8,128)(2,1)}, f32[16,16]{1,0:T(8,128)}, f32[16,16]{1,0:T(8,128)}) custom-call(bf16[1,256,512]{2,1,0:T(8,128)(2,1)S(1)} %get-tuple-element.6.refs_0_, f32[16,16]{1,0:T(8,128)S(1)} %get-tuple-element.7.refs_1_, f32[16,16]{1,0:T(8,128)S(1)} %get-tuple-element.8.refs_2_), custom_call_target="tpu_custom_call" | custom-call | tf_op jit(solution)/shard_map/pallas_call | solution.py:372

commit v4 on v3

--- a/solution.py
+++ b/solution.py
@@ -12,7 +12,7 @@
 F32 = jnp.float32
 BF16 = jnp.bfloat16
 LANES = 128
-OWNERS = 4
+OWNERS = 8
 HIGH = lax.Precision.HIGHEST
 
 
@@ -102,18 +102,16 @@
         greet(barrier, "ctx", me, parts)
         greet(barrier, "dp", row_of, batch)
 
+    eye = iota((modes, modes), 0) == iota((modes, modes), 1)
+
+    def columns(src, dst):
+        for g in range(groups):
+            column = jnp.sum(jnp.where(eye, src[g : g + 1, :], 0.0), axis=1, keepdims=True)
+            dst[g * modes : (g + 1) * modes, :] = jnp.broadcast_to(column, (modes, LANES))
+
     loads[0].wait()
-    loads[1].wait()
     dec = decv[...]
-    series = dec * dec
-    series = 1.0 + series / 6.0 * (1.0 + series / 20.0 * (1.0 + series / 42.0 * (1.0 + series / 72.0)))
-    norm = jnp.sqrt(2.0 * jnp.exp(-dec) * dec * series)
-    eye = iota((modes, modes), 0) == iota((modes, modes), 1)
-    for g in range(groups):
-        at = slice(g * modes, (g + 1) * modes)
-        for src, dst in ((dec, dcol), (resv[...] * norm, rcol)):
-            column = jnp.sum(jnp.where(eye, src[g : g + 1, :], 0.0), axis=1, keepdims=True)
-            dst[at, :] = jnp.broadcast_to(column, (modes, LANES))
+    columns(dec, dcol)
 
     lane_pos = iota((modes, width), 1).astype(F32)
     back_pos = width - lane_pos
@@ -154,51 +152,64 @@
         xrev[:, at] = nn(xv[:, at], anti).astype(BF16)
     lane = iota((LANES, LANES), 1)
     sub = iota((LANES, LANES), 0)
-    later = lane >= sub
+    wanted = (lane < sub) | (lane == LANES - 1)
     low = iota((modes, LANES), 1) % per_group < per_group // 2
+    lane_chunk = iota((modes, LANES), 1) // per_group
+    near = iota((modes, LANES), 1).astype(F32)
+
+    def stack(ref, at):
+        return jnp.concatenate([ref[at, j * LANES : (j + 1) * LANES] for j in range(chunks)], axis=0)
+
+    def both(ref, at, start):
+        return jnp.concatenate(
+            [ref[at, start : start + LANES], ref[at, width + start : width + start + LANES]], axis=1
+        )
+
     for g in range(groups):
         at = slice(g * per_group, (g + 1) * per_group)
-        left = jnp.concatenate([gv[at, j * LANES : (j + 1) * LANES] for j in range(chunks)], axis=0)
-        right = jnp.concatenate(
-            [
-                jnp.concatenate(
-                    [
-                        xrev[at, (j - b) * LANES : (j - b + 1) * LANES] if b <= j else jnp.zeros((per_group, LANES), BF16)
-                        for b in range(chunks)
-                    ],
-                    axis=1,
-                )
-                for j in range(chunks)
-            ],
+        turned = pltpu.roll(tn(stack(gv, at), stack(xrev, at)), 0, axis=1, stride=1, stride_axis=0)
+        lagv[g : g + 1, :] = jnp.sum(jnp.where(wanted, turned, 0.0), axis=0, keepdims=True)
+    for g in range(groups):
+        at = slice(g * modes, (g + 1) * modes)
+        second = slice(rows + g * modes, rows + (g + 1) * modes)
+        chans = slice(g * per_group, (g + 1) * per_group)
+        weights = jnp.concatenate(
+            [both(lg, at, 0), both(lg, second, 0), both(lx, at, width - LANES), both(lx, second, width - LANES)],
             axis=0,
         )
-        pairs = tn(left, right)
-        turned = [
-            pltpu.roll(pairs[:, b * LANES : (b + 1) * LANES], 0, axis=1, stride=1, stride_axis=0)
-            for b in range(chunks)
-        ]
-        zero = jnp.zeros((LANES, LANES), F32)
-        for b in range(chunks + 1):
-            here = turned[b] if b < chunks else zero
-            before = turned[b - 1] if b > 0 else zero
-            lagv[g : g + 1, b * LANES : (b + 1) * LANES] = jnp.sum(jnp.where(later, here, before), axis=0, keepdims=True)
-    zero_lane = iota((groups, LANES), 1) == 0
-    lags = [pltpu.roll(lagv[:, b * LANES : (b + 1) * LANES], 1, axis=1) for b in range(chunks + 1)]
-    lags = jnp.concatenate([jnp.where(zero_lane, lags[b], lags[b + 1]) for b in range(chunks)], axis=1)
-    for g in range(groups):
-        at = slice(g * modes, (g + 1) * modes)
-        e = fwd[at, :] * lags[g : g + 1, :]
-        w = e * lane_pos
-        e = sum(e[:, b * LANES : (b + 1) * LANES] for b in range(chunks))
-        w = sum(w[:, b * LANES : (b + 1) * LANES] for b in range(chunks))
+        data = jnp.concatenate([stack(gv, chans), stack(xv, chans)], axis=0)
+        o = nt(weights, jnp.concatenate([data, data], axis=1))
+        gs, gt = o[:modes], o[modes : 2 * modes]
+        xs, xt = (pltpu.roll(o[j * modes : (j + 1) * modes], LANES // 2, axis=1) for j in (2, 3))
+        lam = jnp.exp(-(dcol[at, :] * float(LANES)))
+        factor, r, rt = 1.0, 0.0, 0.0
+        for n in range(1, chunks):
+            known = lane_chunk < chunks - n
+            a = jnp.where(known, pltpu.roll(gs, LANES - n * per_group, axis=1), 0.0)
+            at_n = jnp.where(known, pltpu.roll(gt, LANES - n * per_group, axis=1), 0.0)
+            r = r + factor * a
+            rt = rt + factor * (at_n + float((n - 1) * LANES) * a)
+            factor = factor * lam
+        e = fwd[at, :LANES] * pltpu.roll(lagv[g : g + 1, :], 1, axis=1)
+        w = e * near + (xs * rt + xt * r)
+        e = e + xs * r
         for shift in (64, 32, 16, 8):
             e = e + pltpu.roll(e, shift, axis=1)
             w = w + pltpu.roll(w, shift, axis=1)
-        both = jnp.where(low, e, w)
+        mixed = jnp.where(low, e, w)
         for h in range(modes // 8):
             k = g * (modes // 8) + h
-            sendl[k // share, k % share : k % share + 1, :] = jnp.sum(jnp.where(own_segment, both[h * 8 : (h + 1) * 8], 0.0), axis=0, keepdims=True)
+            sendl[k // share, k % share : k % share + 1, :] = jnp.sum(
+                jnp.where(own_segment, mixed[h * 8 : (h + 1) * 8], 0.0), axis=0, keepdims=True
+            )
     gather(sendl, recvl, sl, rl)
+
+    loads[1].wait()
+    series = dec * dec
+    series = 1.0 + series / 6.0 * (1.0 + series / 20.0 * (1.0 + series / 42.0 * (1.0 + series / 72.0)))
+    norm = jnp.sqrt(2.0 * jnp.exp(-dec) * dec * series)
+    columns(resv[...] * norm, rcol)
+    later = lane >= sub
 
     for g in range(groups):
         at = slice(g * modes, (g + 1) * modes)
@@ -356,7 +367,7 @@
             vm((rows, width), F32), vm((rows, width), F32),
             vm((2 * rows, chans), F32), vm((2 * rows, chans), F32),
             vm((2 * rows, width), BF16), vm((groups, width + LANES), F32),
-            vm((chans, width), BF16), vm((groups, width + LANES), F32),
+            vm((chans, width), BF16), vm((groups, LANES), F32),
             vm((chans, width), F32), vm((rows, chans), F32),
             vm((owners, share, 4, LANES), F32), vm((parts, share, 4, LANES), F32),
             vm((owners, share, LANES), F32), vm((parts, share, LANES), F32),

time: 30.8 us -> 29.9 us (0.971)
  Pallas kernels: 30 us -> 29.2 us
    pallas_call x1, Pallas kernels: 29.3 us -> 28.4 us  [on_device(): pl.pallas_call(functools.partial(kernel, dims), out_shape=tuple((vm(shape...]
where the time goes in v4:
time: 29.9 us; the launch traced here: 29.8 us
  Pallas kernels  29.2 us (98%)
  between operations  0.64 us (2%)
    pallas_call x1, Pallas kernels, on_device(): pl.pallas_call(functools.partial(kernel, dims), out_shape=tuple((vm(shape...  28.4 us
    pallas_call x1, Pallas kernels, on_device(): pl.pallas_call(finish, out_shape=shapes, in_specs=[pl.BlockSpec(memory_sp...  0.74 us

profile of v4, /device:TPU:1, one launch (start us, length us, event | category | flops | bytes accessed | tf_op | source)
XLA Modules:
  0.0 29.8 jit_solution(11773388449999141559)
XLA Ops:
  0.6 28.4 %shard_map.67 = (bf16[1,256,512]{2,1,0:T(8,128)(2,1)S(1)}, f32[16,16]{1,0:T(8,128)S(1)}, f32[16,16]{1,0:T(8,128)S(1)}) custom-call(bf16[1,256,512]{2,1,0:T(8,128)(2,1)} %x_hbm.1, bf16[1,256,512]{2,1,0:T(8,128)(2,1)} %g_hbm.1, f32[16,16]{1,0:T(8,128)} %res_hbm.1, f32[16,16]{1,0:T(8,128)} %dec_hbm.1), custom_call_target="tpu_custom_call" | custom-call | tf_op jit(solution)/shard_map/pallas_call | solution.py:358
  29.1 0.7 %shard_map.68 = (bf16[1,256,512]{2,1,0:T(8,128)(2,1)}, f32[16,16]{1,0:T(8,128)}, f32[16,16]{1,0:T(8,128)}) custom-call(bf16[1,256,512]{2,1,0:T(8,128)(2,1)S(1)} %get-tuple-element.6.refs_0_, f32[16,16]{1,0:T(8,128)S(1)} %get-tuple-element.7.refs_1_, f32[16,16]{1,0:T(8,128)S(1)} %get-tuple-element.8.refs_2_), custom_call_target="tpu_custom_call" | custom-call | tf_op jit(solution)/shard_map/pallas_call | solution.py:383

commit v5 on v4

--- a/solution.py
+++ b/solution.py
@@ -68,7 +68,7 @@
 
 def kernel(
     dims, x_hbm, g_hbm, res_hbm, dec_hbm, outv, pv, qv,
-    xv, gv, resv, decv, dcol, rcol, lg, lx, fwd, bwd, yg, yx, wout, hrow, xrev, lagv, outl, rx,
+    xv, gv, resv, decv, dcol, rcol, wts, fwd, parts_of, wout, hrow, xrev, lagv, outl, rx,
     send1, recv1, sendl, recvl, send2, recv2, send3, recv3, send4, recv4,
     in_sem, s1, r1, sl, rl, s2, r2, s3, r3, s4, r4,
 ):
@@ -113,34 +113,49 @@
     dec = decv[...]
     columns(dec, dcol)
 
-    lane_pos = iota((modes, width), 1).astype(F32)
-    back_pos = width - lane_pos
+    lane = iota((modes, LANES), 1)
+    near = lane.astype(F32)
+    away = LANES - near
     for g in range(groups):
         at = slice(g * modes, (g + 1) * modes)
-        second = slice(rows + g * modes, rows + (g + 1) * modes)
-        d = jnp.concatenate([dcol[at, :]] * chunks, axis=1)
-        for pos, keep, dst in ((lane_pos, fwd, lg), (back_pos, bwd, lx)):
-            e = jnp.exp(-(d * pos))
-            keep[at, :] = e
-            dst[at, :width], dst[at, width:] = split(e)
-            dst[second, :width], dst[second, width:] = split(e * pos)
+        e = jnp.exp(-(dcol[at, :] * near))
+        f = jnp.exp(-(dcol[at, :] * away))
+        fwd[at, :] = e
+        for kind, value in enumerate((e, e * near, f, f * away)):
+            r0 = (4 * g + kind) * modes
+            wts[r0 : r0 + modes, :LANES], wts[r0 : r0 + modes, LANES:] = split(value)
 
     loads[2].wait()
-    yg[...] = nt(lg[...], jnp.concatenate([gv[...], gv[...]], axis=1))
     loads[3].wait()
-    yx[...] = nt(lx[...], jnp.concatenate([xv[...], xv[...]], axis=1))
+
+    def stack(ref, at):
+        return jnp.concatenate([ref[at, j * LANES : (j + 1) * LANES] for j in range(chunks)], axis=0)
 
     segment = iota((8, LANES), 1) // per_group
     own_segment = segment == iota((8, LANES), 0)
     turned_segment = [segment == (iota((8, LANES), 0) + seg) % 8 for seg in range(8)]
-    for k in range(parts):
-        first = (k * 8 // modes) * per_group
-        half, seg = first // LANES, (first % LANES) // per_group
-        for kind, src in enumerate((yg, yg, yx, yx)):
-            r0 = (kind % 2) * rows + k * 8
-            v = src[r0 : r0 + 8, half * LANES : (half + 1) * LANES]
-            v = pltpu.roll(v, 0, axis=1, stride=per_group, stride_axis=0)
-            send1[k // share, k % share, kind : kind + 1, :] = jnp.sum(jnp.where(turned_segment[seg], v, 0.0), axis=0, keepdims=True)
+    is_grad = lane < chunks * per_group
+    steps = jnp.where(is_grad, lane // per_group, 2 * chunks - 1 - lane // per_group).astype(F32) * float(LANES)
+    for g in range(groups):
+        at = slice(g * modes, (g + 1) * modes)
+        chans = slice(g * per_group, (g + 1) * per_group)
+        data = jnp.concatenate([stack(gv, chans), stack(xv, chans)], axis=0)
+        o = nt(wts[4 * g * modes : 4 * (g + 1) * modes, :], jnp.concatenate([data, data], axis=1))
+        parts_of[4 * g * modes : 4 * (g + 1) * modes, :] = o
+        factor = jnp.exp(-(dcol[at, :] * steps))
+        gs, gt, xs, xt = (o[kind * modes : (kind + 1) * modes] for kind in range(4))
+        for kind, (mask, v) in enumerate(
+            ((is_grad, gs), (is_grad, gt + steps * gs), (~is_grad, xs), (~is_grad, xt + steps * xs))
+        ):
+            v = jnp.where(mask, v * factor, 0.0)
+            for shift in (64, 32, 16):
+                v = v + pltpu.roll(v, shift, axis=1)
+            for h in range(modes // 8):
+                k = g * (modes // 8) + h
+                seg = g % (LANES // per_group)
+                send1[k // share, k % share, kind : kind + 1, :] = jnp.sum(
+                    jnp.where(turned_segment[seg], v[h * 8 : (h + 1) * 8], 0.0), axis=0, keepdims=True
+                )
 
     pl.when(is_owner)(lambda: pl.semaphore_wait(barrier, owners - 1 + batch - 1))
     pl.when(plain)(lambda: pl.semaphore_wait(barrier, owners))
@@ -150,20 +165,11 @@
     for i in range(chunks):
         at = slice(i * LANES, (i + 1) * LANES)
         xrev[:, at] = nn(xv[:, at], anti).astype(BF16)
-    lane = iota((LANES, LANES), 1)
+    square_lane = iota((LANES, LANES), 1)
     sub = iota((LANES, LANES), 0)
-    wanted = (lane < sub) | (lane == LANES - 1)
-    low = iota((modes, LANES), 1) % per_group < per_group // 2
-    lane_chunk = iota((modes, LANES), 1) // per_group
-    near = iota((modes, LANES), 1).astype(F32)
-
-    def stack(ref, at):
-        return jnp.concatenate([ref[at, j * LANES : (j + 1) * LANES] for j in range(chunks)], axis=0)
-
-    def both(ref, at, start):
-        return jnp.concatenate(
-            [ref[at, start : start + LANES], ref[at, width + start : width + start + LANES]], axis=1
-        )
+    wanted = (square_lane < sub) | (square_lane == LANES - 1)
+    low = lane % per_group < per_group // 2
+    lane_chunk = lane // per_group
 
     for g in range(groups):
         at = slice(g * per_group, (g + 1) * per_group)
@@ -171,14 +177,7 @@
         lagv[g : g + 1, :] = jnp.sum(jnp.where(wanted, turned, 0.0), axis=0, keepdims=True)
     for g in range(groups):
         at = slice(g * modes, (g + 1) * modes)
-        second = slice(rows + g * modes, rows + (g + 1) * modes)
-        chans = slice(g * per_group, (g + 1) * per_group)
-        weights = jnp.concatenate(
-            [both(lg, at, 0), both(lg, second, 0), both(lx, at, width - LANES), both(lx, second, width - LANES)],
-            axis=0,
-        )
-        data = jnp.concatenate([stack(gv, chans), stack(xv, chans)], axis=0)
-        o = nt(weights, jnp.concatenate([data, data], axis=1))
+        o = parts_of[4 * g * modes : 4 * (g + 1) * modes, :]
         gs, gt = o[:modes], o[modes : 2 * modes]
         xs, xt = (pltpu.roll(o[j * modes : (j + 1) * modes], LANES // 2, axis=1) for j in (2, 3))
         lam = jnp.exp(-(dcol[at, :] * float(LANES)))
@@ -190,7 +189,7 @@
             r = r + factor * a
             rt = rt + factor * (at_n + float((n - 1) * LANES) * a)
             factor = factor * lam
-        e = fwd[at, :LANES] * pltpu.roll(lagv[g : g + 1, :], 1, axis=1)
+        e = fwd[at, :] * pltpu.roll(lagv[g : g + 1, :], 1, axis=1)
         w = e * near + (xs * rt + xt * r)
         e = e + xs * r
         for shift in (64, 32, 16, 8):
@@ -209,11 +208,13 @@
     series = 1.0 + series / 6.0 * (1.0 + series / 20.0 * (1.0 + series / 42.0 * (1.0 + series / 72.0)))
     norm = jnp.sqrt(2.0 * jnp.exp(-dec) * dec * series)
     columns(resv[...] * norm, rcol)
-    later = lane >= sub
+    later = square_lane >= sub
+    back_pos = width - iota((modes, width), 1).astype(F32)
 
     for g in range(groups):
         at = slice(g * modes, (g + 1) * modes)
-        w = jnp.concatenate([rcol[at, :]] * chunks, axis=1) * bwd[at, :]
+        w = jnp.exp(-(jnp.concatenate([dcol[at, :]] * chunks, axis=1) * back_pos))
+        w = jnp.concatenate([rcol[at, :]] * chunks, axis=1) * w
         wout[at, :], wout[rows + g * modes : rows + (g + 1) * modes, :] = split(w)
         hrow[g : g + 1, :width] = jnp.sum(w, axis=0, keepdims=True)
         start = jnp.sum(rcol[at, :], axis=0, keepdims=True)
@@ -363,9 +364,7 @@
         scratch_shapes=[
             vm((chans, width), BF16), vm((chans, width), BF16), vm((groups, modes), F32), vm((groups, modes), F32),
             vm((rows, LANES), F32), vm((rows, LANES), F32),
-            vm((2 * rows, 2 * width), BF16), vm((2 * rows, 2 * width), BF16),
-            vm((rows, width), F32), vm((rows, width), F32),
-            vm((2 * rows, chans), F32), vm((2 * rows, chans), F32),
+            vm((4 * rows, 2 * LANES), BF16), vm((rows, LANES), F32), vm((4 * rows, LANES), F32),
             vm((2 * rows, width), BF16), vm((groups, width + LANES), F32),
             vm((chans, width), BF16), vm((groups, LANES), F32),
             vm((chans, width), F32), vm((rows, chans), F32),

time: 29.9 us -> 28.8 us (0.963)
  Pallas kernels: 29.2 us -> 28.1 us
    pallas_call x1, Pallas kernels: 28.4 us -> 27.3 us  [on_device(): pl.pallas_call(functools.partial(kernel, dims), out_shape=tuple((vm(shape...]
where the time goes in v5:
time: 28.8 us; the launch traced here: 28.7 us
  Pallas kernels  28.1 us (98%)
  between operations  0.64 us (2%)
    pallas_call x1, Pallas kernels, on_device(): pl.pallas_call(functools.partial(kernel, dims), out_shape=tuple((vm(shape...  27.3 us
    pallas_call x1, Pallas kernels, on_device(): pl.pallas_call(finish, out_shape=shapes, in_specs=[pl.BlockSpec(memory_sp...  0.74 us

profile of v5, /device:TPU:1, one launch (start us, length us, event | category | flops | bytes accessed | tf_op | source)
XLA Modules:
  0.0 28.7 jit_solution(9455353828220791454)
XLA Ops:
  0.6 27.3 %shard_map.67 = (bf16[1,256,512]{2,1,0:T(8,128)(2,1)S(1)}, f32[16,16]{1,0:T(8,128)S(1)}, f32[16,16]{1,0:T(8,128)S(1)}) custom-call(bf16[1,256,512]{2,1,0:T(8,128)(2,1)} %x_hbm.1, bf16[1,256,512]{2,1,0:T(8,128)(2,1)} %g_hbm.1, f32[16,16]{1,0:T(8,128)} %res_hbm.1, f32[16,16]{1,0:T(8,128)} %dec_hbm.1), custom_call_target="tpu_custom_call" | custom-call | tf_op jit(solution)/shard_map/pallas_call | solution.py:359
  28.0 0.7 %shard_map.68 = (bf16[1,256,512]{2,1,0:T(8,128)(2,1)}, f32[16,16]{1,0:T(8,128)}, f32[16,16]{1,0:T(8,128)}) custom-call(bf16[1,256,512]{2,1,0:T(8,128)(2,1)S(1)} %get-tuple-element.6.refs_0_, f32[16,16]{1,0:T(8,128)S(1)} %get-tuple-element.7.refs_1_, f32[16,16]{1,0:T(8,128)S(1)} %get-tuple-element.8.refs_2_), custom_call_target="tpu_custom_call" | custom-call | tf_op jit(solution)/shard_map/pallas_call | solution.py:382

commit v6 on v5

--- a/solution.py
+++ b/solution.py
@@ -69,7 +69,7 @@
 def kernel(
     dims, x_hbm, g_hbm, res_hbm, dec_hbm, outv, pv, qv,
     xv, gv, resv, decv, dcol, rcol, wts, fwd, parts_of, wout, hrow, xrev, lagv, outl, rx,
-    send1, recv1, sendl, recvl, send2, recv2, send3, recv3, send4, recv4,
+    send1, recv1, sendl, recvl, send2, recv2, send3, recv3, send4, recv4, spread,
     in_sem, s1, r1, sl, rl, s2, r2, s3, r3, s4, r4,
 ):
     parts, batch, groups, modes, per_group, width, scale = dims
@@ -84,14 +84,19 @@
     is_owner = me % (parts // 2) < run
     plain = jnp.logical_not(is_owner)
 
-    def gather(src, dst, send_sem, recv_sem):
-        for o, to in enumerate(owner_ids):
+    def gather(src, dst, send_sem, recv_sem, some=slice(None)):
+        for o, to in list(enumerate(owner_ids))[some]:
             pl.when(me != to)(functools.partial(send, src.at[o], dst.at[me], send_sem, recv_sem, "ctx", to))
 
 
     loads = []
     for i, (src, dst) in enumerate(
-        ((dec_hbm, decv), (res_hbm, resv), (g_hbm.at[0], gv), (x_hbm.at[0], xv))
+        [(dec_hbm, decv), (res_hbm, resv)]
+        + [
+            (src.at[0, pl.ds(h * LANES, LANES)], dst.at[pl.ds(h * LANES, LANES)])
+            for h in range(groups * per_group // LANES)
+            for src, dst in ((g_hbm, gv), (x_hbm, xv))
+        ]
     ):
         loads.append(pltpu.make_async_copy(src, dst, in_sem.at[i]))
         loads[-1].start()
@@ -125,9 +130,6 @@
             r0 = (4 * g + kind) * modes
             wts[r0 : r0 + modes, :LANES], wts[r0 : r0 + modes, LANES:] = split(value)
 
-    loads[2].wait()
-    loads[3].wait()
-
     def stack(ref, at):
         return jnp.concatenate([ref[at, j * LANES : (j + 1) * LANES] for j in range(chunks)], axis=0)
 
@@ -139,6 +141,13 @@
     for g in range(groups):
         at = slice(g * modes, (g + 1) * modes)
         chans = slice(g * per_group, (g + 1) * per_group)
+        if 2 * g == groups:
+            pl.when(is_owner)(lambda: pl.semaphore_wait(barrier, owners - 1 + batch - 1))
+            pl.when(plain)(lambda: pl.semaphore_wait(barrier, owners))
+            gather(send1, recv1, s1, r1, slice(0, owners // 2))
+        if chans.start % LANES == 0:
+            for load in loads[2 + 2 * (chans.start // LANES) :][:2]:
+                load.wait()
         data = jnp.concatenate([stack(gv, chans), stack(xv, chans)], axis=0)
         o = nt(wts[4 * g * modes : 4 * (g + 1) * modes, :], jnp.concatenate([data, data], axis=1))
         parts_of[4 * g * modes : 4 * (g + 1) * modes, :] = o
@@ -157,9 +166,7 @@
                     jnp.where(turned_segment[seg], v[h * 8 : (h + 1) * 8], 0.0), axis=0, keepdims=True
                 )
 
-    pl.when(is_owner)(lambda: pl.semaphore_wait(barrier, owners - 1 + batch - 1))
-    pl.when(plain)(lambda: pl.semaphore_wait(barrier, owners))
-    gather(send1, recv1, s1, r1)
+    gather(send1, recv1, s1, r1, slice(owners // 2, None))
 
     anti = (iota((LANES, LANES), 0) + iota((LANES, LANES), 1) == LANES - 1).astype(BF16)
     for i in range(chunks):
@@ -252,17 +259,21 @@
     def _():
         recv1[pl.ds(me, 1)] = send1[pl.ds(slot, 1)]
         recvl[pl.ds(me, 1)] = sendl[pl.ds(slot, 1)]
-        all_wait(recv1.at[pl.ds(0, parts - 1)], r1)
         first_half = iota((1, LANES), 1) % per_group < per_group // 2
+        factors = []
         for j in range(share):
             k = slot * share + j
             seg = k * 8 // modes % (LANES // per_group)
             mine = dcol[pl.ds(pl.multiple_of(k * 8, 8), 8), :]
             dl = jnp.sum(jnp.where(segment == (iota((8, LANES), 0) + seg) % 8, mine, 0.0), axis=0, keepdims=True)
+            factors.append({1 << i: jnp.exp(-(dl * float(width << i))) for i in range(parts.bit_length() - 1)})
+        all_wait(recv1.at[pl.ds(0, parts - 1)], r1)
+        for j in range(share):
+            seg = (slot * share + j) * 8 // modes % (LANES // per_group)
             gs, gt, xs, xt = (recv1[:, j, kind, :] for kind in range(4))
             n = 1
             while n < parts:
-                factor = jnp.exp(-(dl * float(n * width)))
+                factor = factors[j][n]
                 ahead = down(gs, n)
                 gt = gt + factor * (down(gt, n) + float(n * width) * ahead)
                 gs = gs + factor * ahead
@@ -309,13 +320,13 @@
     same_mode = from_lane // per_group == to_lane % 8
     kind_of = (from_lane % per_group >= per_group // 2) == (to_lane >= LANES // 2)
     select = jnp.where(same_mode & kind_of & (to_lane % (LANES // 2) < modes), 1.0, 0.0)
-    fold = (iota((groups, parts), 0) == iota((groups, parts), 1) // 2).astype(F32)
     pl.when(is_owner)(lambda: all_wait(recv4.at[pl.ds(0, owners - 1)], r4))
     pl.when(plain)(lambda: all_wait(recv4, r4))
     sums = jnp.concatenate([recv4[o] for o in range(owners)], axis=0)
     sums = jnp.dot(sums, select, precision=HIGH, preferred_element_type=F32)
     sums = jnp.where(iota((parts, LANES), 0) % 2 == iota((parts, LANES), 1) % modes // 8, sums, 0.0)
-    total = jnp.dot(fold, sums, precision=HIGH, preferred_element_type=F32)
+    spread[...] = sums
+    total = spread[pl.ds(0, groups, stride=2), :] + spread[pl.ds(1, groups, stride=2), :]
     pv[...] = total[:, :modes] * (norm * scale)
     qv[...] = total[:, LANES // 2 : LANES // 2 + modes] * (dec * norm * scale)
 
@@ -372,8 +383,8 @@
             vm((owners, share, LANES), F32), vm((parts, share, LANES), F32),
             vm((parts, share, LANES), F32), vm((owners, share, LANES), F32),
             vm((share, LANES), F32), vm((batch, share, LANES), F32),
-            vm((share, LANES), F32), vm((owners, share, LANES), F32),
-            pltpu.SemaphoreType.DMA((4,)),
+            vm((share, LANES), F32), vm((owners, share, LANES), F32), vm((rows // 8, LANES), F32),
+            pltpu.SemaphoreType.DMA((2 + 2 * (chans // LANES),)),
         ] + [pltpu.SemaphoreType.DMA] * 10,
         compiler_params=pltpu.CompilerParams(
             collective_id=0, has_side_effects=True, vmem_limit_bytes=60 * 1024 * 1024

time: 28.8 us -> 28.7 us (level)
  no operation moved by 1% of the time
where the time goes in v6:
time: 28.7 us; the launch traced here: 28.6 us
  Pallas kernels  27.9 us (97%)
  between operations  0.64 us (2%)
    pallas_call x1, Pallas kernels, on_device(): pl.pallas_call(functools.partial(kernel, dims), out_shape=tuple((vm(shape...  27.2 us
    pallas_call x1, Pallas kernels, on_device(): pl.pallas_call(finish, out_shape=shapes, in_specs=[pl.BlockSpec(memory_sp...  0.74 us

profile of v6, /device:TPU:1, one launch (start us, length us, event | category | flops | bytes accessed | tf_op | source)
XLA Modules:
  0.0 28.6 jit_solution(5660960237874462146)
XLA Ops:
  0.6 27.2 %shard_map.67 = (bf16[1,256,512]{2,1,0:T(8,128)(2,1)S(1)}, f32[16,16]{1,0:T(8,128)S(1)}, f32[16,16]{1,0:T(8,128)S(1)}) custom-call(bf16[1,256,512]{2,1,0:T(8,128)(2,1)} %x_hbm.1, bf16[1,256,512]{2,1,0:T(8,128)(2,1)} %g_hbm.1, f32[16,16]{1,0:T(8,128)} %res_hbm.1, f32[16,16]{1,0:T(8,128)} %dec_hbm.1), custom_call_target="tpu_custom_call" | custom-call | tf_op jit(solution)/shard_map/pallas_call | solution.py:370
  27.8 0.7 %shard_map.68 = (bf16[1,256,512]{2,1,0:T(8,128)(2,1)}, f32[16,16]{1,0:T(8,128)}, f32[16,16]{1,0:T(8,128)}) custom-call(bf16[1,256,512]{2,1,0:T(8,128)(2,1)S(1)} %get-tuple-element.6.refs_0_, f32[16,16]{1,0:T(8,128)S(1)} %get-tuple-element.7.refs_1_, f32[16,16]{1,0:T(8,128)S(1)} %get-tuple-element.8.refs_2_), custom_call_target="tpu_custom_call" | custom-call | tf_op jit(solution)/shard_map/pallas_call | solution.py:393

commit v7 on v6

--- a/solution.py
+++ b/solution.py
@@ -13,7 +13,6 @@
 BF16 = jnp.bfloat16
 LANES = 128
 OWNERS = 8
-HIGH = lax.Precision.HIGHEST
 
 
 def iota(shape, dim):
@@ -323,7 +322,8 @@
     pl.when(is_owner)(lambda: all_wait(recv4.at[pl.ds(0, owners - 1)], r4))
     pl.when(plain)(lambda: all_wait(recv4, r4))
     sums = jnp.concatenate([recv4[o] for o in range(owners)], axis=0)
-    sums = jnp.dot(sums, select, precision=HIGH, preferred_element_type=F32)
+    select = select.astype(BF16)
+    sums = nn(jnp.concatenate(split(sums), axis=1), jnp.concatenate([select, select], axis=0))
     sums = jnp.where(iota((parts, LANES), 0) % 2 == iota((parts, LANES), 1) % modes // 8, sums, 0.0)
     spread[...] = sums
     total = spread[pl.ds(0, groups, stride=2), :] + spread[pl.ds(1, groups, stride=2), :]

time: 28.7 us -> 28.6 us (level)
  no operation moved by 1% of the time
where the time goes in v7:
time: 28.6 us; the launch traced here: 28.5 us
  Pallas kernels  27.9 us (98%)
  between operations  0.64 us (2%)
    pallas_call x1, Pallas kernels, on_device(): pl.pallas_call(functools.partial(kernel, dims), out_shape=tuple((vm(shape...  27.1 us
    pallas_call x1, Pallas kernels, on_device(): pl.pallas_call(finish, out_shape=shapes, in_specs=[pl.BlockSpec(memory_sp...  0.74 us

profile of v7, /device:TPU:1, one launch (start us, length us, event | category | flops | bytes accessed | tf_op | source)
XLA Modules:
  0.0 28.5 jit_solution(12973518191878359659)
XLA Ops:
  0.6 27.1 %shard_map.67 = (bf16[1,256,512]{2,1,0:T(8,128)(2,1)S(1)}, f32[16,16]{1,0:T(8,128)S(1)}, f32[16,16]{1,0:T(8,128)S(1)}) custom-call(bf16[1,256,512]{2,1,0:T(8,128)(2,1)} %x_hbm.1, bf16[1,256,512]{2,1,0:T(8,128)(2,1)} %g_hbm.1, f32[16,16]{1,0:T(8,128)} %res_hbm.1, f32[16,16]{1,0:T(8,128)} %dec_hbm.1), custom_call_target="tpu_custom_call" | custom-call | tf_op jit(solution)/shard_map/pallas_call | solution.py:370
  27.8 0.7 %shard_map.68 = (bf16[1,256,512]{2,1,0:T(8,128)(2,1)}, f32[16,16]{1,0:T(8,128)}, f32[16,16]{1,0:T(8,128)}) custom-call(bf16[1,256,512]{2,1,0:T(8,128)(2,1)S(1)} %get-tuple-element.6.refs_0_, f32[16,16]{1,0:T(8,128)S(1)} %get-tuple-element.7.refs_1_, f32[16,16]{1,0:T(8,128)S(1)} %get-tuple-element.8.refs_2_), custom_call_target="tpu_custom_call" | custom-call | tf_op jit(solution)/shard_map/pallas_call | solution.py:393
